TPU v7x, 32 devices: a whole 2x2x4 slice. The times are simulated.
32 devices in a mesh: wide: 8 (over y, x, core), narrow: 4 (over z).
Axes of the slice: x: 2, y: 2, z: 4, core: 2. Of those that a mesh axis runs over, the one named last changes fastest.
Arguments:
- images: bfloat16 [3, 1024000], P(None, ('wide', 'narrow')), may hold values from -6 to 6
- large_flag: int32 [640], P(('wide', 'narrow')), may hold values from 0 to 1
- labels: int32 [640], P(('wide', 'narrow')), may hold values from 0 to 9
- example_weights: int32 [640], P(('wide', 'narrow')), may hold values from 1 to 6
- cycle_noise: int32 [8, 7, 28056], P('wide'), may hold values from 0 to 65535
- stem_weight: float32 [64, 27], P('wide'), may hold values from -1.25 to 1.25
- conv_weight: float32 [6, 64, 576], P(None, 'wide'), may hold values from -0.25 to 0.25
- norm_params: float32 [2, 7, 64], P(None, None, 'wide'), as said below
- head_weight: float32 [10, 64], P(None, 'wide'), may hold values from -3 to 3
- head_bias: float32 [10], replicated, may hold values from -3 to 3
- stem_first: float32 [64, 27], P('wide'), may hold values from -6.67572e-06 to 6.67572e-06
- stem_second: float32 [64, 27], P('wide'), may hold values from 1.7820706e-14 to 7.1282823e-14
- conv_first: float32 [6, 64, 576], P(None, 'wide'), may hold values from -6.67572e-06 to 6.67572e-06
- conv_second: float32 [6, 64, 576], P(None, 'wide'), may hold values from 1.7820706e-14 to 7.1282823e-14
- norm_first: float32 [2, 7, 64], P(None, None, 'wide'), may hold values from -6.67572e-06 to 6.67572e-06
- norm_second: float32 [2, 7, 64], P(None, None, 'wide'), may hold values from 1.7820706e-14 to 7.1282823e-14
- head_first: float32 [10, 64], P(None, 'wide'), may hold values from -6.67572e-06 to 6.67572e-06
- head_second: float32 [10, 64], P(None, 'wide'), may hold values from 1.7820706e-14 to 7.1282823e-14
- bias_first: float32 [10], replicated, may hold values from -6.67572e-06 to 6.67572e-06
- bias_second: float32 [10], replicated, may hold values from 1.7820706e-14 to 7.1282823e-14
Outputs:
- stem_new: float32 [64, 27], P('wide')
- stem_first_new: float32 [64, 27], P('wide')
- stem_second_new: float32 [64, 27], P('wide')
- conv_new: float32 [6, 64, 576], P(None, 'wide')
- conv_first_new: float32 [6, 64, 576], P(None, 'wide')
- conv_second_new: float32 [6, 64, 576], P(None, 'wide')
- norm_new: float32 [2, 7, 64], P(None, None, 'wide')
- norm_first_new: float32 [2, 7, 64], P(None, None, 'wide')
- norm_second_new: float32 [2, 7, 64], P(None, None, 'wide')
- head_new: float32 [10, 64], P(None, 'wide')
- head_first_new: float32 [10, 64], P(None, 'wide')
- head_second_new: float32 [10, 64], P(None, 'wide')
- bias_new: float32 [10], replicated
- bias_first_new: float32 [10], replicated
- bias_second_new: float32 [10], replicated
- grad_norm: float32 [], replicated
- loss_sum: float32 [], replicated
- weight_total: float32 [], replicated
Inputs may be any that keep to these rules, and one draw needn't show every extreme that they name: `norm_params`: gains of the batch norms in row 0 are positive.
All inputs are finite; a program needn't handle non-finite values. Where the computation divides by a largest or mean magnitude, that divisor is 1e-20 or more.
Results may differ from a plain program's by a relative error of at most 0.025.
Values may be sent and summed in bfloat16 or wider, within the bound.
No kernel may reach another device: no remote copies, remote signals or barrier semaphores. Data moves between devices by JAX's collectives and lax.ppermute only.
A program may use at most 960 MiB of HBM per device.

v0:
```python
import jax
import jax.numpy as jnp
from jax import lax
from jax.sharding import PartitionSpec as P

SIDE = 40
SHORT = 32
STEP = 10


norm_epsilon = 1e-05
clip_limit = 0.002
learn_rate = 0.4
first_decay = 0.9
second_decay = 0.999
adam_epsilon = 1e-08
weight_decay = 0.0005
decoupled = 0.01
levels = 15.0


def passed_along(value, axis, by):
    count = lax.axis_size(axis)
    return lax.ppermute(value, axis, [(i, (i + by) % count) for i in range(count)])


def tap_masks(pixels):
    position = jnp.arange(pixels, dtype=jnp.int32) % (SIDE * SIDE)
    row_index = position // SIDE
    col_index = position % SIDE
    tables = []
    for tap in range(9):
        row_step = tap // 3 - 1
        col_step = tap % 3 - 1
        inside = (
            (row_index + row_step >= 0)
            & (row_index + row_step < SIDE)
            & (col_index + col_step >= 0)
            & (col_index + col_step < SIDE)
        )
        tables.append(inside)
    return jnp.stack(tables, 0).astype(jnp.bfloat16)


def unfold(field, tap_table):
    pixels = field.shape[1]
    margin = SIDE + 1
    padded = jnp.pad(field, ((0, 0), (margin, margin)))
    pieces = []
    for tap in range(9):
        offset = (tap // 3 - 1) * SIDE + tap % 3 - 1
        pieces.append(
            padded[:, margin + offset : margin + offset + pixels] * tap_table[tap][None, :]
        )
    return jnp.concatenate(pieces, 0)


def fold_back(columns, tap_table, inputs):
    pixels = columns.shape[1]
    margin = SIDE + 1
    total = jnp.zeros((inputs, pixels), jnp.float32)
    for tap in range(9):
        offset = (tap // 3 - 1) * SIDE + tap % 3 - 1
        piece = columns[tap * inputs : (tap + 1) * inputs] * tap_table[tap][None, :].astype(
            jnp.float32
        )
        total = (
            total
            + jnp.pad(piece, ((0, 0), (margin + offset, margin - offset)))[
                :, margin : margin + pixels
            ]
        )
    return total


def conv_apply(field_low, matrix_low, tap_table):
    return jnp.dot(matrix_low, unfold(field_low, tap_table), preferred_element_type=jnp.float32)


def conv_backward(grad_low, inputs_low, matrix_low, tap_table):
    columns = unfold(inputs_low, tap_table)
    weight_grad = lax.dot_general(
        grad_low, columns, (((1,), (1,)), ((), ())), preferred_element_type=jnp.float32
    )
    back_columns = lax.dot_general(
        matrix_low, grad_low, (((0,), (0,)), ((), ())), preferred_element_type=jnp.float32
    )
    return (weight_grad, fold_back(back_columns, tap_table, inputs_low.shape[0]))


def norm_forward(conv_out, gain, shift, pixel_mask, pixel_total):
    masked = conv_out * pixel_mask
    sums, squares = lax.psum(
        (jnp.sum(masked, 1), jnp.sum(masked * conv_out, 1)), ("wide", "narrow")
    )
    mean = sums / pixel_total
    scale = lax.rsqrt(squares / pixel_total - mean * mean + norm_epsilon)
    normed = (conv_out - mean[:, None]) * scale[:, None]
    return (normed * gain[:, None] + shift[:, None], normed, scale)


def norm_backward(grad_out, normed, scale, gain, pixel_mask, pixel_total):
    shift_local = jnp.sum(grad_out, 1)
    gain_local = jnp.sum(grad_out * normed, 1)
    shift_total, gain_total = lax.psum((shift_local, gain_local), ("wide", "narrow"))
    grad_in = (
        (gain * scale)[:, None]
        * (
            grad_out
            - shift_total[:, None] / pixel_total
            - normed * gain_total[:, None] / pixel_total
        )
        * pixel_mask
    )
    return (grad_in, gain_local, shift_local)


def silu_grad(value):
    sigma = jax.nn.sigmoid(value)
    return sigma * (1.0 + value * (1.0 - sigma))


def flatten(stem, conv, norm, head, pieces):
    width = stem.shape[0] // pieces
    return jnp.concatenate(
        [
            stem.reshape(pieces, -1),
            conv.reshape(6, pieces, width, -1).transpose(1, 0, 2, 3).reshape(pieces, -1),
            norm.reshape(2, 7, pieces, width).transpose(2, 0, 1, 3).reshape(pieces, -1),
            head.reshape(head.shape[0], pieces, width).transpose(1, 0, 2).reshape(pieces, -1),
        ],
        1,
    )


def unflatten_one(share, width, channels, classes):
    first = width * 27
    second = first + 6 * width * 9 * channels
    third = second + 14 * width
    return (
        share[:first].reshape(width, 27),
        share[first:second].reshape(6, width, 9 * channels),
        share[second:third].reshape(2, 7, width),
        share[third:].reshape(classes, width),
    )


def quantize(block_value, noise):
    scale = jnp.max(jnp.abs(block_value), axis=-1, keepdims=True) + 1e-06
    dither = (noise.astype(jnp.float32) + 0.5) / 65536.0 - 0.5
    return (block_value / scale * levels + dither, scale)


def adam_update(gradient, first, second, master, factor):
    clipped = gradient * factor
    new_first = first_decay * first + (1.0 - first_decay) * clipped
    new_second = second_decay * second + (1.0 - second_decay) * clipped * clipped
    corrected = (
        new_first
        / (1.0 - first_decay**STEP)
        / (jnp.sqrt(new_second / (1.0 - second_decay**STEP)) + adam_epsilon)
    )
    return (master - learn_rate * (corrected + decoupled * master), new_first, new_second)


def body(
    images,
    large_flag,
    labels,
    example_weights,
    cycle_noise,
    stem_weight,
    conv_weight,
    norm_params,
    head_weight,
    head_bias,
    stem_first,
    stem_second,
    conv_first,
    conv_second,
    norm_first,
    norm_second,
    head_first,
    head_second,
    bias_first,
    bias_second,
):
    conv_full, stem_full, head_full = (
        lax.all_gather(conv_weight.astype(jnp.bfloat16), "wide", axis=1, tiled=True),
        lax.all_gather(stem_weight.astype(jnp.bfloat16), "wide", axis=0, tiled=True),
        lax.all_gather(head_weight.astype(jnp.bfloat16), "wide", axis=1, tiled=True),
    )
    norm_full = lax.all_gather(norm_params, "wide", axis=2, tiled=True)
    count = large_flag.shape[0]
    area = SIDE * SIDE
    pixels = count * area
    channels = stem_full.shape[0]
    classes = head_full.shape[0]
    sides = jnp.where(large_flag == 1, SIDE, SHORT).astype(jnp.int32)
    position = jnp.arange(area, dtype=jnp.int32)
    valid = ((position // SIDE)[None, :] < sides[:, None]) & (
        (position % SIDE)[None, :] < sides[:, None]
    )
    pixel_mask = valid.astype(jnp.float32).reshape(1, pixels)
    pixel_counts = (sides * sides).astype(jnp.float32)
    weights_f = example_weights.astype(jnp.float32)
    pixel_total, weight_total = lax.psum(
        (jnp.sum(pixel_mask), jnp.sum(weights_f)), ("wide", "narrow")
    )
    tap_table = tap_masks(pixels)
    planes = images * pixel_mask.astype(jnp.bfloat16)
    stem_out = conv_apply(planes, stem_full, tap_table)
    stem_pre, stem_normed, stem_scale = norm_forward(
        stem_out, norm_full[0, 0], norm_full[1, 0], pixel_mask, pixel_total
    )
    stream = jax.nn.silu(stem_pre) * pixel_mask
    saved = []
    for index in range(3):
        inputs_low = stream.astype(jnp.bfloat16)
        first_out = conv_apply(inputs_low, conv_full[2 * index], tap_table)
        first_pre, first_normed, first_scale = norm_forward(
            first_out,
            norm_full[0, 1 + 2 * index],
            norm_full[1, 1 + 2 * index],
            pixel_mask,
            pixel_total,
        )
        hidden_low = (jax.nn.silu(first_pre) * pixel_mask).astype(jnp.bfloat16)
        second_out = conv_apply(hidden_low, conv_full[2 * index + 1], tap_table)
        second_pre, second_normed, second_scale = norm_forward(
            second_out,
            norm_full[0, 2 + 2 * index],
            norm_full[1, 2 + 2 * index],
            pixel_mask,
            pixel_total,
        )
        second_pre = second_pre + stream
        saved.append(
            (
                inputs_low,
                first_pre,
                first_normed,
                first_scale,
                hidden_low,
                second_pre,
                second_normed,
                second_scale,
            )
        )
        stream = jax.nn.silu(second_pre) * pixel_mask
    pooled = jnp.sum(stream.reshape(channels, count, area), 2) / pixel_counts[None, :]
    pooled_low = pooled.astype(jnp.bfloat16)
    logits = (
        jnp.dot(pooled_low.T, head_full.T, preferred_element_type=jnp.float32) + head_bias[None, :]
    )
    shifted = logits - jnp.max(logits, axis=1, keepdims=True)
    log_total = jnp.log(jnp.sum(jnp.exp(shifted), axis=1))
    onehot = (labels[:, None] == jnp.arange(classes, dtype=jnp.int32)[None, :]).astype(jnp.float32)
    losses = log_total - jnp.sum(onehot * shifted, axis=1)
    loss_part = jnp.sum(weights_f * losses)
    probs = jnp.exp(shifted - log_total[:, None])
    grad_logits = ((weights_f / weight_total)[:, None] * (probs - onehot)).astype(jnp.bfloat16)
    bias_grad = jnp.sum(grad_logits.astype(jnp.float32), 0)
    head_grad = jnp.dot(grad_logits.T, pooled_low.T, preferred_element_type=jnp.float32)
    grad_pooled = jnp.dot(head_full.T, grad_logits.T, preferred_element_type=jnp.float32)
    grad_stream = jnp.broadcast_to(
        (grad_pooled / pixel_counts[None, :])[:, :, None], (channels, count, area)
    ).reshape(channels, pixels)
    conv_grads = [None] * 6
    gain_grads = [None] * 7
    shift_grads = [None] * 7
    for index in reversed(range(3)):
        (
            inputs_low,
            first_pre,
            first_normed,
            first_scale,
            hidden_low,
            second_pre,
            second_normed,
            second_scale,
        ) = saved[index]
        grad_second = grad_stream * pixel_mask * silu_grad(second_pre)
        grad_conv, gain_grads[2 + 2 * index], shift_grads[2 + 2 * index] = norm_backward(
            grad_second,
            second_normed,
            second_scale,
            norm_full[0, 2 + 2 * index],
            pixel_mask,
            pixel_total,
        )
        conv_grads[2 * index + 1], grad_hidden = conv_backward(
            grad_conv.astype(jnp.bfloat16), hidden_low, conv_full[2 * index + 1], tap_table
        )
        grad_first = grad_hidden * pixel_mask * silu_grad(first_pre)
        grad_conv, gain_grads[1 + 2 * index], shift_grads[1 + 2 * index] = norm_backward(
            grad_first,
            first_normed,
            first_scale,
            norm_full[0, 1 + 2 * index],
            pixel_mask,
            pixel_total,
        )
        conv_grads[2 * index], grad_inputs = conv_backward(
            grad_conv.astype(jnp.bfloat16), inputs_low, conv_full[2 * index], tap_table
        )
        grad_stream = grad_second + grad_inputs
    grad_stem = grad_stream * pixel_mask * silu_grad(stem_pre)
    grad_conv, gain_grads[0], shift_grads[0] = norm_backward(
        grad_stem, stem_normed, stem_scale, norm_full[0, 0], pixel_mask, pixel_total
    )
    stem_grad = lax.dot_general(
        grad_conv.astype(jnp.bfloat16),
        unfold(planes, tap_table),
        (((1,), (1,)), ((), ())),
        preferred_element_type=jnp.float32,
    )
    conv_grad = jnp.stack(conv_grads, 0)
    norm_grad = jnp.stack([jnp.stack(gain_grads, 0), jnp.stack(shift_grads, 0)], 0)
    wide_count = lax.axis_size("wide")
    member = lax.axis_index("wide")
    flat = flatten(stem_grad, conv_grad, norm_grad, head_grad, wide_count)
    flat, bias_sum, loss_narrow = (
        lax.psum(flat.astype(jnp.bfloat16), "narrow").astype(jnp.float32),
        lax.psum(bias_grad.astype(jnp.bfloat16), "narrow").astype(jnp.float32),
        lax.psum(loss_part.astype(jnp.bfloat16), "narrow").astype(jnp.float32),
    )

    def own_row(row):
        piece = lax.dynamic_index_in_dim(flat, (row + 2 * wide_count) % wide_count, 0, False)
        return piece

    def one_hop(hop, carried):
        noise = lax.dynamic_index_in_dim(cycle_noise[0], hop - 1, 0, False)
        level, scale = quantize(carried, noise)
        level_in = passed_along(level.astype(jnp.bfloat16), "wide", 1)
        scale_in = passed_along(scale, "wide", 1)
        return level_in.astype(jnp.float32) * scale_in / levels + own_row(member - 1 - hop)

    reduced = lax.fori_loop(1, wide_count, one_hop, own_row(member - 1))
    stem_share, conv_share, norm_share, head_share = unflatten_one(
        reduced, stem_weight.shape[0], channels, classes
    )
    stem_share = stem_share + weight_decay * stem_weight
    conv_share = conv_share + weight_decay * conv_weight
    head_share = head_share + weight_decay * head_weight
    squares = (
        jnp.sum(stem_share * stem_share)
        + jnp.sum(conv_share * conv_share)
        + jnp.sum(norm_share * norm_share)
        + jnp.sum(head_share * head_share)
    )
    square_total, bias_total, loss_total = lax.psum((squares, bias_sum, loss_narrow), "wide")
    grad_norm = jnp.sqrt(square_total + jnp.sum(bias_total * bias_total))
    factor = clip_limit / jnp.maximum(grad_norm, clip_limit)
    stem_new, stem_first_new, stem_second_new = adam_update(
        stem_share, stem_first, stem_second, stem_weight, factor
    )
    conv_new, conv_first_new, conv_second_new = adam_update(
        conv_share, conv_first, conv_second, conv_weight, factor
    )
    norm_new, norm_first_new, norm_second_new = adam_update(
        norm_share, norm_first, norm_second, norm_params, factor
    )
    head_new, head_first_new, head_second_new = adam_update(
        head_share, head_first, head_second, head_weight, factor
    )
    bias_new, bias_first_new, bias_second_new = adam_update(
        bias_total, bias_first, bias_second, head_bias, factor
    )
    return (
        stem_new,
        stem_first_new,
        stem_second_new,
        conv_new,
        conv_first_new,
        conv_second_new,
        norm_new,
        norm_first_new,
        norm_second_new,
        head_new,
        head_first_new,
        head_second_new,
        bias_new,
        bias_first_new,
        bias_second_new,
        grad_norm,
        loss_total,
        weight_total,
    )


def solution(mesh):
    return jax.shard_map(
        body,
        mesh=mesh,
        in_specs=(
            P(None, ("wide", "narrow")),
            P(("wide", "narrow")),
            P(("wide", "narrow")),
            P(("wide", "narrow")),
            P("wide", None, None),
            P("wide", None),
            P(None, "wide", None),
            P(None, None, "wide"),
            P(None, "wide"),
            P(),
            P("wide", None),
            P("wide", None),
            P(None, "wide", None),
            P(None, "wide", None),
            P(None, None, "wide"),
            P(None, None, "wide"),
            P(None, "wide"),
            P(None, "wide"),
            P(),
            P(),
        ),
        out_specs=(
            P("wide", None),
            P("wide", None),
            P("wide", None),
            P(None, "wide", None),
            P(None, "wide", None),
            P(None, "wide", None),
            P(None, None, "wide"),
            P(None, None, "wide"),
            P(None, None, "wide"),
            P(None, "wide"),
            P(None, "wide"),
            P(None, "wide"),
            P(),
            P(),
            P(),
            P(),
            P(),
            P(),
        ),
        check_vma=False,
    )
```

profile of v0, /device:TPU:0, one launch (start us, length us, event | category | flops | bytes accessed | tf_op | source)
XLA Modules:
  0.0 2056.4 jit_solution(11856435640756742150)
XLA Ops:
  89.8 40.2 %all-reduce.68 = (f32[64]{0:T(128)S(1)}, f32[]{:T(128)}, f32[64]{0:T(128)S(1)}) all-reduce(f32[64]{0:T(128)S(1)} %get-tuple-element.365, f32[]{:T(128)} %fusion.88, f32[64]{0:T(128)S(1)} %get-tuple-element.364), channel_id=1, replica_groups=mesh['wide'=8,'narrow'=4] {'wide','narrow'}, use_global_device_ids=true, to_apply=%region_5.6 | all-reduce | flops 129 | bytes 1032 | tf_op jit(solution)/shard_map/psum | solution.py:93
  197.7 39.6 %all-reduce.67 = (f32[64]{0:T(128)S(1)}, f32[64]{0:T(128)S(1)}) all-reduce(f32[64]{0:T(128)S(1)} %get-tuple-element.363, f32[64]{0:T(128)S(1)} %get-tuple-element.362), channel_id=1, replica_groups=mesh['wide'=8,'narrow'=4] {'wide','narrow'}, use_global_device_ids=true, to_apply=%region_9.10 | all-reduce | flops 128 | bytes 1024 | tf_op jit(solution)/shard_map/psum | solution.py:93
  294.2 39.1 %all-reduce.66 = (f32[64]{0:T(128)S(1)}, f32[64]{0:T(128)S(1)}) all-reduce(f32[64]{0:T(128)S(1)} %get-tuple-element.361, f32[64]{0:T(128)S(1)} %get-tuple-element.360), channel_id=1, replica_groups=mesh['wide'=8,'narrow'=4] {'wide','narrow'}, use_global_device_ids=true, to_apply=%region_13.14 | all-reduce | flops 128 | bytes 1024 | tf_op jit(solution)/shard_map/psum | solution.py:93
  394.1 41.0 %all-reduce.65 = (f32[64]{0:T(128)S(1)}, f32[64]{0:T(128)S(1)}) all-reduce(f32[64]{0:T(128)S(1)} %get-tuple-element.359, f32[64]{0:T(128)S(1)} %get-tuple-element.358), channel_id=1, replica_groups=mesh['wide'=8,'narrow'=4] {'wide','narrow'}, use_global_device_ids=true, to_apply=%region_17.18 | all-reduce | flops 128 | bytes 1024 | tf_op jit(solution)/shard_map/psum | solution.py:93
  491.6 39.2 %all-reduce.64 = (f32[64]{0:T(128)S(1)}, f32[64]{0:T(128)S(1)}) all-reduce(f32[64]{0:T(128)S(1)} %get-tuple-element.357, f32[64]{0:T(128)S(1)} %get-tuple-element.356), channel_id=1, replica_groups=mesh['wide'=8,'narrow'=4] {'wide','narrow'}, use_global_device_ids=true, to_apply=%region_21.22 | all-reduce | flops 128 | bytes 1024 | tf_op jit(solution)/shard_map/psum | solution.py:93
  590.7 41.0 %all-reduce.63 = (f32[64]{0:T(128)S(1)}, f32[64]{0:T(128)S(1)}) all-reduce(f32[64]{0:T(128)S(1)} %get-tuple-element.355, f32[64]{0:T(128)S(1)} %get-tuple-element.354), channel_id=1, replica_groups=mesh['wide'=8,'narrow'=4] {'wide','narrow'}, use_global_device_ids=true, to_apply=%region_25.26 | all-reduce | flops 128 | bytes 1024 | tf_op jit(solution)/shard_map/psum | solution.py:93
  688.5 39.6 %all-reduce.62 = (f32[64]{0:T(128)S(1)}, f32[64]{0:T(128)S(1)}) all-reduce(f32[64]{0:T(128)S(1)} %get-tuple-element.353, f32[64]{0:T(128)S(1)} %get-tuple-element.352), channel_id=1, replica_groups=mesh['wide'=8,'narrow'=4] {'wide','narrow'}, use_global_device_ids=true, to_apply=%region_29.30 | all-reduce | flops 128 | bytes 1024 | tf_op jit(solution)/shard_map/psum | solution.py:93
  765.9 39.4 %psum.255 = f32[]{:T(128)} all-reduce(f32[]{:T(128)} %get-tuple-element.406), channel_id=1, replica_groups=mesh['wide'=8,'narrow'=4] {'wide','narrow'}, use_global_device_ids=true, to_apply=%region_7.8 | all-reduce | flops 1 | bytes 8 | tf_op jit(solution)/shard_map/psum | solution.py:207
  836.4 39.9 %all-reduce.61 = (f32[64]{0:T(128)S(1)}, f32[64]{0:T(128)S(1)}) all-reduce(f32[64]{0:T(128)S(1)} %get-tuple-element.379, f32[64]{0:T(128)S(1)} %get-tuple-element.378), channel_id=1, replica_groups=mesh['wide'=8,'narrow'=4] {'wide','narrow'}, use_global_device_ids=true, to_apply=%region_38.39 | all-reduce | flops 128 | bytes 1024 | tf_op jit(solution)/shard_map/psum | solution.py:105
  886.2 28.1 %convolution_bitcast_fusion.5 = f32[576,32000]{1,0:T(8,128)} fusion(bf16[64,32000]{1,0:T(8,128)(2,1)} %multiply_convert_fusion.6, bf16[6,64,576]{2,1,0:T(8,128)(2,1)S(1)} %all_gather.14), kind=kOutput, calls=%fused_computation.10 | convolution fusion | flops 2359296000 | bytes 77905920 | tf_op jit(solution)/shard_map/dot_general | solution.py:85
  914.3 42.7 %slice_multiply_fusion.53 = (f32[64,32000]{1,0:T(8,128)}, f32[64,32000]{1,0:T(8,128)}, f32[64,32000]{1,0:T(8,128)}, f32[64,32000]{1,0:T(8,128)}, f32[64,32000]{1...) fusion(f32[576,32000]{1,0:T(8,128)} %convolution_bitcast_fusion.5, ...), kind=kLoop, calls=%fused_computation.203 | loop fusion | flops 16384000 | bytes 132096000 | tf_op jit(solution)/shard_map/mul | solution.py:64
  957.0 32.5 %fusion.109 = (f32[64]{0:T(128)S(1)}, f32[64]{0:T(128)S(1)}, f32[64,32000]{1,0:T(8,128)}) fusion(f32[64]{0:T(128)S(1)} %get-tuple-element.493, f32[64,32000]{1,0:T(8,128)} %get-tuple-element.572, f32[64]{0:T(128)S(1)} %get-tuple-element.494, f32[64]{0:T(128)S(1)} %copy-done.43, f32[64]{0:T(128)S(1)} %copy-done.26, f32[32000]{0:T(1024)S(1)} %reshape.485, ...), kind=kLoop, calls=%fused_computation.495 | loop fusion | flops 51199872 | bytes 90369536 | tf_op jit(solution)/shard_map/reduce_sum | solution.py:103
  990.1 40.7 %all-reduce.60 = (f32[64]{0:T(128)S(1)}, f32[64]{0:T(128)S(1)}) all-reduce(f32[64]{0:T(128)S(1)} %get-tuple-element.377, f32[64]{0:T(128)S(1)} %get-tuple-element.376), channel_id=1, replica_groups=mesh['wide'=8,'narrow'=4] {'wide','narrow'}, use_global_device_ids=true, to_apply=%region_42.43 | all-reduce | flops 128 | bytes 1024 | tf_op jit(solution)/shard_map/psum | solution.py:105
  1068.8 42.7 %slice_multiply_fusion.44 = (f32[64,32000]{1,0:T(8,128)}, f32[64,32000]{1,0:T(8,128)}, f32[64,32000]{1,0:T(8,128)}, f32[64,32000]{1,0:T(8,128)}, f32[64,32000]{1...) fusion(f32[576,32000]{1,0:T(8,128)} %convolution_bitcast_fusion.4, ...), kind=kLoop, calls=%fused_computation.194 | loop fusion | flops 16384000 | bytes 132096000 | tf_op jit(solution)/shard_map/mul | solution.py:64
  1111.5 37.3 %fusion.108 = (f32[64]{0:T(128)S(1)}, f32[64]{0:T(128)S(1)}, f32[64,32000]{1,0:T(8,128)}) fusion(f32[64]{0:T(128)S(1)} %copy-done.36, f32[64,32000]{1,0:T(8,128)} %get-tuple-element.571, f32[64]{0:T(128)S(1)} %copy-done.38, f32[64,32000]{1,0:T(8,128)} %get-tuple-element.503, f32[32000]{0:T(1024)S(1)} %reshape.485, f32[64,32000]{1,0:T(8,128)} %get-tuple-element.499, ...), kind=kLoop, calls=%fused_computation.494 | loop fusion | flops 49151872 | bytes 106753024 | tf_op jit(solution)/shard_map/reduce_sum | solution.py:103
  1149.4 39.8 %all-reduce.59 = (f32[64]{0:T(128)S(1)}, f32[64]{0:T(128)S(1)}) all-reduce(f32[64]{0:T(128)S(1)} %get-tuple-element.375, f32[64]{0:T(128)S(1)} %get-tuple-element.374), channel_id=1, replica_groups=mesh['wide'=8,'narrow'=4] {'wide','narrow'}, use_global_device_ids=true, to_apply=%region_46.47 | all-reduce | flops 128 | bytes 1024 | tf_op jit(solution)/shard_map/psum | solution.py:105
  1199.0 28.1 %convolution_bitcast_fusion.3 = f32[576,32000]{1,0:T(8,128)} fusion(bf16[64,32000]{1,0:T(8,128)(2,1)} %multiply_convert_fusion.4, bf16[6,64,576]{2,1,0:T(8,128)(2,1)S(1)} %all_gather.14), kind=kOutput, calls=%fused_computation.8 | convolution fusion | flops 2359296000 | bytes 77905920 | tf_op jit(solution)/shard_map/dot_general | solution.py:85
  1227.2 42.7 %slice_multiply_fusion.35 = (f32[64,32000]{1,0:T(8,128)}, f32[64,32000]{1,0:T(8,128)}, f32[64,32000]{1,0:T(8,128)}, f32[64,32000]{1,0:T(8,128)}, f32[64,32000]{1...) fusion(f32[576,32000]{1,0:T(8,128)} %convolution_bitcast_fusion.3, ...), kind=kLoop, calls=%fused_computation.185 | loop fusion | flops 16384000 | bytes 132096000 | tf_op jit(solution)/shard_map/mul | solution.py:64
  1269.9 32.4 %fusion.107 = (f32[64]{0:T(128)S(1)}, f32[64]{0:T(128)S(1)}, f32[64,32000]{1,0:T(8,128)}) fusion(f32[64]{0:T(128)S(1)} %copy-done.28, f32[64,32000]{1,0:T(8,128)} %get-tuple-element.570, f32[64]{0:T(128)S(1)} %copy-done.30, f32[64]{0:T(128)S(1)} %copy-done.42, f32[64]{0:T(128)S(1)} %copy-done.25, f32[32000]{0:T(1024)S(1)} %reshape.485, ...), kind=kLoop, calls=%fused_computation.493 | loop fusion | flops 51199872 | bytes 90369536 | tf_op jit(solution)/shard_map/reduce_sum | solution.py:103
  1302.9 40.7 %all-reduce.58 = (f32[64]{0:T(128)S(1)}, f32[64]{0:T(128)S(1)}) all-reduce(f32[64]{0:T(128)S(1)} %get-tuple-element.373, f32[64]{0:T(128)S(1)} %get-tuple-element.372), channel_id=1, replica_groups=mesh['wide'=8,'narrow'=4] {'wide','narrow'}, use_global_device_ids=true, to_apply=%region_50.51 | all-reduce | flops 128 | bytes 1024 | tf_op jit(solution)/shard_map/psum | solution.py:105
  1353.4 28.1 %convolution_bitcast_fusion.2 = f32[576,32000]{1,0:T(8,128)} fusion(bf16[64,32000]{1,0:T(8,128)(2,1)} %multiply_convert_fusion.3, bf16[6,64,576]{2,1,0:T(8,128)(2,1)S(1)} %all_gather.14), kind=kOutput, calls=%fused_computation.7 | convolution fusion | flops 2359296000 | bytes 77905920 | tf_op jit(solution)/shard_map/dot_general | solution.py:85
  1381.6 42.6 %slice_multiply_fusion.26 = (f32[64,32000]{1,0:T(8,128)}, f32[64,32000]{1,0:T(8,128)}, f32[64,32000]{1,0:T(8,128)}, f32[64,32000]{1,0:T(8,128)}, f32[64,32000]{1...) fusion(f32[576,32000]{1,0:T(8,128)} %convolution_bitcast_fusion.2, ...), kind=kLoop, calls=%fused_computation.176 | loop fusion | flops 16384000 | bytes 132096000 | tf_op jit(solution)/shard_map/mul | solution.py:64
  1424.2 37.3 %fusion.106 = (f32[64]{0:T(128)S(1)}, f32[64]{0:T(128)S(1)}, f32[64,32000]{1,0:T(8,128)}) fusion(f32[64]{0:T(128)S(1)} %copy-done.32, f32[64,32000]{1,0:T(8,128)} %get-tuple-element.569, f32[64]{0:T(128)S(1)} %copy-done.34, f32[64,32000]{1,0:T(8,128)} %get-tuple-element.505, f32[32000]{0:T(1024)S(1)} %reshape.485, f32[64,32000]{1,0:T(8,128)} %get-tuple-element.491, ...), kind=kLoop, calls=%fused_computation.492 | loop fusion | flops 49151872 | bytes 106753024 | tf_op jit(solution)/shard_map/reduce_sum | solution.py:103
  1462.0 39.6 %all-reduce.57 = (f32[64]{0:T(128)S(1)}, f32[64]{0:T(128)S(1)}) all-reduce(f32[64]{0:T(128)S(1)} %get-tuple-element.371, f32[64]{0:T(128)S(1)} %get-tuple-element.370), channel_id=1, replica_groups=mesh['wide'=8,'narrow'=4] {'wide','narrow'}, use_global_device_ids=true, to_apply=%region_54.55 | all-reduce | flops 128 | bytes 1024 | tf_op jit(solution)/shard_map/psum | solution.py:105
  1511.5 28.1 %convolution_bitcast_fusion.1 = f32[576,32000]{1,0:T(8,128)} fusion(bf16[64,32000]{1,0:T(8,128)(2,1)} %multiply_convert_fusion.2, bf16[6,64,576]{2,1,0:T(8,128)(2,1)S(1)} %all_gather.14), kind=kOutput, calls=%fused_computation.6 | convolution fusion | flops 2359296000 | bytes 77905920 | tf_op jit(solution)/shard_map/dot_general | solution.py:85
  1539.6 42.7 %slice_multiply_fusion.17 = (f32[64,32000]{1,0:T(8,128)}, f32[64,32000]{1,0:T(8,128)}, f32[64,32000]{1,0:T(8,128)}, f32[64,32000]{1,0:T(8,128)}, f32[64,32000]{1...) fusion(f32[576,32000]{1,0:T(8,128)} %convolution_bitcast_fusion.1, ...), kind=kLoop, calls=%fused_computation.167 | loop fusion | flops 16384000 | bytes 132096000 | tf_op jit(solution)/shard_map/mul | solution.py:64
  1582.4 32.6 %fusion.105 = (f32[64]{0:T(128)S(1)}, f32[64]{0:T(128)S(1)}, f32[64,32000]{1,0:T(8,128)}) fusion(f32[64]{0:T(128)S(1)} %copy-done.21, f32[64,32000]{1,0:T(8,128)} %get-tuple-element.568, f32[64]{0:T(128)S(1)} %copy-done.23, f32[64]{0:T(128)S(1)} %copy-done.40, f32[64]{0:T(128)S(1)} %copy-done.19, f32[32000]{0:T(1024)S(1)} %reshape.485, ...), kind=kLoop, calls=%fused_computation.491 | loop fusion | flops 51199872 | bytes 90369536 | tf_op jit(solution)/shard_map/reduce_sum | solution.py:103
  1615.0 41.2 %all-reduce.56 = (f32[64]{0:T(128)S(1)}, f32[64]{0:T(128)S(1)}) all-reduce(f32[64]{0:T(128)S(1)} %get-tuple-element.369, f32[64]{0:T(128)S(1)} %get-tuple-element.368), channel_id=1, replica_groups=mesh['wide'=8,'narrow'=4] {'wide','narrow'}, use_global_device_ids=true, to_apply=%region_58.59 | all-reduce | flops 128 | bytes 1024 | tf_op jit(solution)/shard_map/psum | solution.py:105
  1711.6 42.6 %slice_multiply_fusion.8 = (f32[64,32000]{1,0:T(8,128)}, f32[64,32000]{1,0:T(8,128)}, f32[64,32000]{1,0:T(8,128)}, f32[64,32000]{1,0:T(8,128)}, f32[64,32000]{1,...) fusion(f32[576,32000]{1,0:T(8,128)} %convolution_bitcast_fusion, f32[32000]{0:T(1024)S(1)} %mul.1054, ...), kind=kLoop, calls=%fused_computation.158 | loop fusion | flops 16384000 | bytes 132096000 | tf_op jit(solution)/shard_map/mul | solution.py:64
  1754.3 35.2 %fusion.104 = (f32[64]{0:T(128)S(1)}, f32[64]{0:T(128)S(1)}, f32[64,32000]{1,0:T(8,128)}) fusion(f32[64]{0:T(128)S(1)} %copy-done.15, f32[64,32000]{1,0:T(8,128)} %get-tuple-element.567, f32[64]{0:T(128)S(1)} %copy-done.17, f32[64]{0:T(128)S(1)} %copy-done.13, f32[64]{0:T(128)S(1)} %copy-done.11, f32[32000]{0:T(1024)S(1)} %reshape.485, ...), kind=kLoop, calls=%fused_computation.490 | loop fusion | flops 53247872 | bytes 98561536 | tf_op jit(solution)/shard_map/reduce_sum | solution.py:103
  1789.5 39.5 %all-reduce.55 = (f32[64]{0:T(128)S(1)}, f32[64]{0:T(128)S(1)}) all-reduce(f32[64]{0:T(128)S(1)} %get-tuple-element.367, f32[64]{0:T(128)S(1)} %get-tuple-element.366), channel_id=1, replica_groups=mesh['wide'=8,'narrow'=4] {'wide','narrow'}, use_global_device_ids=true, to_apply=%region_62.63 | all-reduce | flops 128 | bytes 1024 | tf_op jit(solution)/shard_map/psum | solution.py:105
  1968.3 54.7 %while.18 = (s32[]{:T(128)}, f32[28056]{0:T(1024)S(1)}, s32[1,7,28056]{2,0,1:T(1,128)}, s32[]{:T(128)}, f32[8,28056]{1,0:T(8,128)S(1)}, /*index=5*/f32[]{:T(128)...) while((s32[]{:T(128)}, f32[28056]{0:T(1024)S(1)}, ...), condition=%wide.region_66.67_spmd, body=%wide.region_64.66_spmd.sunk | while | flops 392802 | bytes 1234876 | solution.py:340
  (473 shorter events, 854.7 us)
Async XLA Ops:
  7.2 1959.2 %all-reduce.73.cloned.1.call-start = ((), (), s32[]{:S(2)}) async-start(), calls=%async_computation | async-start | bytes 901120 | tf_op jit(solution)/shard_map/psum | solution.py:324
  54.2 202.9 %copy-start.18 = (f32[64]{0:T(128)}, f32[64]{0:T(128)S(1)}, u32[]{:S(2)}) copy-start(f32[64]{0:T(128)S(1)} %get-tuple-element.400) | copy-start | bytes 772
  54.2 280.3 %copy-start.10 = (f32[64]{0:T(128)}, f32[64]{0:T(128)S(1)}, u32[]{:S(2)}) copy-start(f32[64]{0:T(128)S(1)} %get-tuple-element.402) | copy-start | bytes 772
  54.2 280.3 %copy-start.12 = (f32[64]{0:T(128)}, f32[64]{0:T(128)S(1)}, u32[]{:S(2)}) copy-start(f32[64]{0:T(128)S(1)} %get-tuple-element.401) | copy-start | bytes 772
  131.2 203.3 %copy-start.14 = (f32[64]{0:T(128)}, f32[64]{0:T(128)S(1)}, u32[]{:S(2)}) copy-start(f32[64]{0:T(128)S(1)} %get-tuple-element.473) | copy-start | bytes 772
  131.2 203.3 %copy-start.16 = (f32[64]{0:T(128)}, f32[64]{0:T(128)S(1)}, u32[]{:S(2)}) copy-start(f32[64]{0:T(128)S(1)} %get-tuple-element.474) | copy-start | bytes 772
  1926.9 116.9 %copy-start.9 = (f32[2,7,8]{2,0,1:T(2,128)S(1)}, f32[2,7,8]{2,0,1:T(2,128)}, u32[]{:S(2)}) copy-start(f32[2,7,8]{2,0,1:T(2,128)} %param.29) | copy-start | bytes 1348
  1926.9 116.8 %copy-start.44 = (f32[2,7,8]{2,0,1:T(2,128)S(1)}, f32[2,7,8]{2,0,1:T(2,128)}, u32[]{:S(2)}) copy-start(f32[2,7,8]{2,0,1:T(2,128)} %param.36) | copy-start | bytes 1348
  1926.9 116.8 %copy-start.45 = (f32[2,7,8]{2,0,1:T(2,128)S(1)}, f32[2,7,8]{2,0,1:T(2,128)}, u32[]{:S(2)}) copy-start(f32[2,7,8]{2,0,1:T(2,128)} %param.37) | copy-start | bytes 1348
  1927.0 118.7 %copy-start.75 = (f32[10]{0:T(128)S(1)}, f32[10]{0:T(128)}, u32[]{:S(2)}) copy-start(f32[10]{0:T(128)} %param.31) | copy-start | bytes 124
  1927.0 118.7 %copy-start.76 = (f32[10]{0:T(128)S(1)}, f32[10]{0:T(128)}, u32[]{:S(2)}) copy-start(f32[10]{0:T(128)} %param.40) | copy-start | bytes 124
  1927.0 118.7 %copy-start.77 = (f32[10]{0:T(128)S(1)}, f32[10]{0:T(128)}, u32[]{:S(2)}) copy-start(f32[10]{0:T(128)} %param.41) | copy-start | bytes 124
  1927.0 119.2 %copy-start.49 = (f32[10,8]{0,1:T(8,128)S(1)}, f32[10,8]{0,1:T(8,128)}, u32[]{:S(2)}) copy-start(f32[10,8]{0,1:T(8,128)} %param.38) | copy-start | bytes 964
  1927.0 119.2 %copy-start.50 = (f32[10,8]{0,1:T(8,128)S(1)}, f32[10,8]{0,1:T(8,128)}, u32[]{:S(2)}) copy-start(f32[10,8]{0,1:T(8,128)} %param.39) | copy-start | bytes 964
  1927.0 119.8 %copy-start.4 = (f32[6,8,576]{2,1,0:T(8,128)S(1)}, f32[6,8,576]{2,1,0:T(8,128)}, u32[]{:S(2)}) copy-start(f32[6,8,576]{2,1,0:T(8,128)} %param.34) | copy-start | bytes 331780
  1927.0 119.8 %copy-start.5 = (f32[6,8,576]{2,1,0:T(8,128)S(1)}, f32[6,8,576]{2,1,0:T(8,128)}, u32[]{:S(2)}) copy-start(f32[6,8,576]{2,1,0:T(8,128)} %param.35) | copy-start | bytes 331780
  1927.0 120.6 %copy-start.51 = (f32[8,27]{1,0:T(8,128)S(1)}, f32[8,27]{1,0:T(8,128)}, u32[]{:S(2)}) copy-start(f32[8,27]{1,0:T(8,128)} %param.32) | copy-start | bytes 2596
  1927.0 120.6 %copy-start.52 = (f32[8,27]{1,0:T(8,128)S(1)}, f32[8,27]{1,0:T(8,128)}, u32[]{:S(2)}) copy-start(f32[8,27]{1,0:T(8,128)} %param.33) | copy-start | bytes 2596
  1970.3 4.6 collective-permute-start.1
  1970.4 4.5 collective-permute-start
  1978.1 4.6 collective-permute-start.1
  1978.2 4.5 collective-permute-start
  1985.9 4.6 collective-permute-start.1
  1986.0 4.5 collective-permute-start
  1993.7 4.6 collective-permute-start.1
  1993.8 4.5 collective-permute-start
  2001.6 4.6 collective-permute-start.1
  2001.6 4.5 collective-permute-start
  2009.4 4.6 collective-permute-start.1
  2009.5 4.5 collective-permute-start
  2017.2 4.6 collective-permute-start.1
  2017.3 4.5 collective-permute-start
  (75 other events, 3287.2 us)
Sparse Core Ops, SparseCore 0:
  1928.6 37.7 all-reduce.72
where the time goes:
time: 2070 us; the launch traced here: 2060 us
  other arithmetic  839 us (41%)
  blocking collectives  666 us (32%)
  matrix products  398 us (19%)
  local copies, waits for them, and re-layouts  71.6 us (3%)
  waiting for transfers between devices  47.8 us (2%)
  between operations  20.8 us (1%)
    psum x7, blocking collectives, norm_backward(): lax.psum((shift_local, gain_local), ('wide', 'narrow'))  281 us
    psum x7, blocking collectives, norm_forward(): lax.psum((jnp.sum(masked, 1), jnp.sum(masked * conv_out, 1)), ('wide', 'n...  280 us
    mul x15, other arithmetic, fold_back(): columns[tap * inputs:(tap + 1) * inputs]  256 us
    reduce_sum x7, other arithmetic, norm_backward(): shift_local = jnp.sum(grad_out, 1)  220 us
    dot_general x6, matrix products, conv_backward(): lax.dot_general(matrix_low, grad_low, (((0,), (0,)), ((), ())), preferred...  169 us
    unnamed x52, other arithmetic  166 us
    dot_general x7, matrix products, conv_apply(): jnp.dot(matrix_low, unfold(field_low, tap_table), preferred_element_type=...  116 us
    dot_general x6, matrix products, conv_backward(): lax.dot_general(grad_low, columns, (((1,), (1,)), ((), ())), preferred_el...  104 us
  transfers between devices with their start and end apart: 15, of which 8 were waited for; matrix products, arithmetic and copies ran while one was open for 0% of the time, Pallas kernels for 0%

commit v1 on v0

v1 whole, which is shorter than its diff:
```python
import functools

import jax
import jax.numpy as jnp
import numpy as np
from jax import lax
from jax.experimental import pallas as pl
from jax.experimental.pallas import tpu as pltpu
from jax.sharding import PartitionSpec as P

SIDE = 40
SHORT = 32
STEP = 10

norm_epsilon = 1e-05
clip_limit = 0.002
learn_rate = 0.4
first_decay = 0.9
second_decay = 0.999
adam_epsilon = 1e-08
weight_decay = 0.0005
decoupled = 0.01
levels = 15.0

QUARTERS = 4
PATCHES = SIDE // 2
NI = PATCHES // QUARTERS
NJ = PATCHES
SHORT_J = SHORT // 2
LANES = 256
UNROLL = 4
LAG = 2
VMEM_LIMIT = 52 * 2**20

f32 = jnp.float32
bf16 = jnp.bfloat16
BOTH = ("wide", "narrow")


def window_place(slot):
    group, sy, sx = slot // 4, (slot // 2) % 2, slot % 2
    wx = 1 + sx if group in (0, 2) else (3 if sx == 0 else 0)
    wy = 1 + sy if group in (0, 1) else (3 if sy == 0 else 0)
    return wy, wx


def tap_of(slot, out):
    wy, wx = window_place(slot)
    ky, kx = wy - out // 2, wx - out % 2
    if 0 <= ky < 3 and 0 <= kx < 3:
        return ky * 3 + kx
    return None


def whole():
    return pl.BlockSpec(memory_space=pltpu.VMEM)


def call(kernel, outs, scratch, args, name, cost=None):
    return pl.pallas_call(
        kernel,
        out_shape=outs,
        in_specs=[whole()] * len(args),
        out_specs=jax.tree.map(lambda _: whole(), outs),
        scratch_shapes=scratch,
        compiler_params=pltpu.CompilerParams(vmem_limit_bytes=VMEM_LIMIT),
        name=name,
        cost_estimate=cost,
    )(*args)


def field(rows):
    return jax.ShapeDtypeStruct((NI, NJ, rows, LANES), bf16)


def wide_pair(row):
    turned = pltpu.roll(row, 64, 1)
    lower = lax.broadcasted_iota(jnp.int32, row.shape, 1) < 64
    first = jnp.where(lower, row, turned)
    second = jnp.where(lower, turned, row)
    return jnp.concatenate([first, first], 1), jnp.concatenate([second, second], 1)


def folded(row):
    half = row[:, :128] + row[:, 128:]
    return half + pltpu.roll(half, 64, 1)


def message(first, second):
    lower = lax.broadcasted_iota(jnp.int32, (1, 128), 1) < 64
    return jnp.where(lower, folded(first), folded(second))


def totals(gathered):
    return wide_pair(jnp.sum(gathered[:, :128], 0, keepdims=True))


def norm_constants(gathered, counted, norm4, index):
    sums, squares = totals(gathered)
    mean = sums / counted
    scale = lax.rsqrt(squares / counted - mean * mean + norm_epsilon)
    gain = norm4[index : index + 1]
    slope = gain * scale
    return mean, scale, slope, norm4[7 + index : 8 + index] - mean * slope


def pixels_of(gathered_first):
    return jnp.sum(gathered_first[:, 128:129], 0, keepdims=True)


def twice(tile):
    return jnp.concatenate([tile, tile], 1)


def mask_row(J):
    return jnp.where(J < SHORT_J, 0, jnp.where(J < NJ, 1, 2))


def put_column(ring, slot, s, value, low, q_ref):
    rows = value.shape[0]
    ring[slot, s + 1] = low
    if s == 0:
        ring[slot, NI + 1, :, :128] = (pltpu.roll(value[:, :128], rows - 1, 0) * q_ref[0]).astype(
            bf16
        )
    if s == NI - 1:
        ring[slot, 0, :, 128:] = (pltpu.roll(value[:, 128:], 1, 0) * q_ref[1]).astype(bf16)


def side_columns(ring, side, u, lanes):
    for s in range(NI + 2):
        if s == 0:
            side[u, s, :, 128:] = jnp.where(
                lanes[:, 128:], ring[u + 2, s, :, 128:], ring[u, s, :, 128:]
            )
        elif s == NI + 1:
            side[u, s, :, :128] = jnp.where(
                lanes[:, :128], ring[u + 2, s, :, :128], ring[u, s, :, :128]
            )
        else:
            side[u, s] = jnp.where(lanes, ring[u + 2, s], ring[u, s])


def operands(ring, side, u):
    rows = ring.shape[2]
    whole_rows = NI * rows
    last = NI + 2
    own = ring[u + 1, 1 : NI + 1].reshape(whole_rows, LANES)
    beside = side[u, 1 : NI + 1].reshape(whole_rows, LANES)
    above = jnp.concatenate(
        [ring[u + 1, 2:last, :, :128], ring[u + 1, 0:NI, :, 128:]], -1
    ).reshape(whole_rows, LANES)
    corner = jnp.concatenate([side[u, 2:last, :, :128], side[u, 0:NI, :, 128:]], -1).reshape(
        whole_rows, LANES
    )
    return own, beside, above, corner


def product(parts, w_ref):
    total = jnp.dot(parts[0], w_ref[0:LANES], preferred_element_type=f32)
    for k in range(1, 4):
        total += jnp.dot(
            parts[k], w_ref[k * LANES : (k + 1) * LANES], preferred_element_type=f32
        )
    return total


def by_eight(value):
    return jnp.sum(value.reshape(value.shape[0] // 8, 8, value.shape[1]), 0)


def half_lanes(rows):
    return lax.broadcasted_iota(jnp.int32, (rows, LANES), 1) % 128 < 64


def weights_kernel(conv_ref, forward_ref, backward_ref):
    for layer in range(6):
        matrix = conv_ref[layer].astype(f32)
        turned = matrix.T
        empty = jnp.zeros((64, 64), f32)
        for slot in range(16):
            ahead, back = [], []
            for out in range(4):
                tap = tap_of(slot, out)
                if tap is None:
                    ahead.append(empty)
                    back.append(empty)
                else:
                    other = 8 - tap
                    ahead.append(turned[tap * 64 : (tap + 1) * 64])
                    back.append(matrix[:, other * 64 : (other + 1) * 64])
            at = slice(slot * 64, (slot + 1) * 64)
            forward_ref[layer, at] = jnp.concatenate(ahead, 1).astype(bf16)
            backward_ref[layer, at] = jnp.concatenate(back, 1).astype(bf16)


def stem_kernel(planes_ref, w_ref, mask_ref, info_ref, out_ref, z_ref, stat_ref, zf, *, devices):
    rows = planes_ref.shape[1]
    zf[...] = jnp.zeros_like(zf)
    span = 2 * NI
    blocks = SIDE // span
    deep = (span + 2) * 4
    for i in range(3):
        turned = planes_ref[i].astype(f32).T
        for block in range(blocks):
            first = max(block * span - 1, 0)
            last = min(block * span + span + 1, SIDE)
            skip = first - (block * span - 1)
            for y in range(span):
                base = (block * (span + 2) + y + 1) * deep + skip * 4 + i
                zf[pl.ds(base, last - first, stride=4), :rows] = turned[
                    y * SIDE + first : y * SIDE + last
                ]
    lane = lax.broadcasted_iota(jnp.int32, (deep, 128), 1)
    for block in range(blocks):
        at = block * (span + 2) * deep
        low = zf[at + span * deep : at + (span + 1) * deep]
        zf[at : at + deep] = jnp.where(lane % 4 == 0, 0.0, pltpu.roll(low, 1, 1))
        high = zf[at + deep : at + 2 * deep]
        zf[at + (span + 1) * deep : at + (span + 2) * deep] = jnp.where(
            lane % 4 == 3, 0.0, pltpu.roll(high, 127, 1)
        )
    z_ref[...] = zf[...].astype(bf16)
    first_sum = jnp.zeros((8, LANES), f32)
    second_sum = jnp.zeros((8, LANES), f32)
    for block in range(blocks):
        for s in range(NI):
            at = (block * (span + 2) + 2 * s) * deep
            result = lax.dot_general(
                z_ref[at : at + 4 * deep],
                w_ref[...],
                (((0,), (0,)), ((), ())),
                preferred_element_type=f32,
            )
            for j in range(NI):
                J = block * NI + j
                mask = mask_ref[0 if J < SHORT_J else 1, 0 if s == 0 else 1]
                tile = result[:rows, j * LANES : (j + 1) * LANES] * twice(mask)
                out_ref[s, J] = tile.astype(bf16)
                first_sum += by_eight(tile)
                second_sum += by_eight(tile * tile)
    row = message(
        jnp.sum(first_sum, 0, keepdims=True), jnp.sum(second_sum, 0, keepdims=True)
    )
    counts = jnp.sum(info_ref[...], 0, keepdims=True) * (1.0 / QUARTERS)
    stat_ref[...] = jnp.broadcast_to(jnp.concatenate([row, counts], 1), (devices, LANES))


def forward_kernel(*refs, index, keep, residual, devices):
    refs = list(refs)
    c_ref = refs.pop(0)
    res_ref = refs.pop(0) if residual else None
    gath_ref, first_ref, norm_ref, mask_ref, q_ref, w_ref, out_ref = refs[:7]
    refs = refs[7:]
    keep_ref = refs.pop(0) if keep else None
    stat_ref, ring, side, sums = refs
    rows = c_ref.shape[2]
    counted = pixels_of(first_ref)
    _, _, slope, start = norm_constants(gath_ref, counted, norm_ref, index)
    half_slope, half_start = slope * 0.5, start * 0.5
    lanes = half_lanes(rows)
    sums[...] = jnp.zeros_like(sums)

    def activate(J, slot):
        Jc = jnp.minimum(J, NJ - 1)
        jm = mask_row(J)
        for s in range(NI):
            half = c_ref[s, Jc].astype(f32) * half_slope + half_start
            if residual:
                half = half + 0.5 * res_ref[s, Jc].astype(f32)
            mask = mask_ref[jm, 0 if s == 0 else 1]
            value = (half + half * jnp.tanh(half)) * twice(mask)
            low = value.astype(bf16)
            put_column(ring, slot, s, value, low, q_ref)
            if keep:
                @pl.when(J < NJ)
                def _():
                    keep_ref[s, Jc] = low

    def convolve(J, u):
        side_columns(ring, side, u, lanes)
        total = product(operands(ring, side, u), w_ref)
        jm = mask_row(J)
        first_sum, second_sum = sums[0], sums[1]
        for s in range(NI):
            tile = total[s * rows : (s + 1) * rows] * twice(mask_ref[jm, 0 if s == 0 else 1])
            out_ref[s, J] = tile.astype(bf16)
            first_sum += by_eight(tile)
            second_sum += by_eight(tile * tile)
        sums[0], sums[1] = first_sum, second_sum

    ring[UNROLL] = jnp.zeros(ring.shape[1:], bf16)
    for k in range(LAG):
        activate(k, UNROLL + 1 + k)

    def step(i, carry):
        for k in range(LAG + 1):
            ring[k] = ring[UNROLL + k]
        for u in range(UNROLL):
            activate(i * UNROLL + u + LAG, u + LAG + 1)
            convolve(i * UNROLL + u, u)
        return carry

    lax.fori_loop(0, NJ // UNROLL, step, 0)
    row = message(jnp.sum(sums[0], 0, keepdims=True), jnp.sum(sums[1], 0, keepdims=True))
    stat_ref[...] = jnp.broadcast_to(row, (devices, 128))


def head_kernel(
    c_ref, res_ref, gath_ref, first_ref, norm_ref, mask_ref, hot_ref, info_ref, into_ref, back_ref,
    bias_ref, dy_ref, stat_ref, head_ref, small_ref, grads, pool, *, classes, devices
):
    rows = c_ref.shape[2]
    counted = pixels_of(first_ref)
    weight_total = jnp.sum(first_ref[:, 129:130], 0, keepdims=True)
    mean, scale, slope, start = norm_constants(gath_ref, counted, norm_ref, 6)
    half_slope, half_start = slope * 0.5, start * 0.5
    pool[...] = jnp.zeros_like(pool)

    def gather(J, carry):
        jm = mask_row(J)
        total = pool[...]
        for s in range(NI):
            half = c_ref[s, J].astype(f32) * half_slope + half_start
            half = half + 0.5 * res_ref[s, J].astype(f32)
            mask = twice(mask_ref[jm, 0 if s == 0 else 1])
            t = jnp.tanh(half)
            total += (half + half * t) * mask
            grads[s, J] = (0.5 + 0.5 * t) * (1.0 + half * (1.0 - t)) * mask
        pool[...] = total
        return carry

    lax.fori_loop(0, NJ, gather, 0)
    pooled = pool[...]
    row_index = lax.broadcasted_iota(jnp.int32, (rows, LANES), 0)
    pooled = pooled + jnp.where(
        row_index % 2 == 0, pltpu.roll(pooled, rows - 1, 0), pltpu.roll(pooled, 1, 0)
    )
    pooled = pooled + jnp.where(
        row_index % 4 < 2, pltpu.roll(pooled, rows - 2, 0), pltpu.roll(pooled, 2, 0)
    )
    half_pool = pooled[:, :128] + pooled[:, 128:]
    half_pool = half_pool + pltpu.roll(half_pool, 64, 1)
    count = info_ref[:, 0:1]
    weight = info_ref[:, 1:2]
    pooled_low = (half_pool / count).astype(bf16)
    logits = jnp.dot(pooled_low, into_ref[...], preferred_element_type=f32) + bias_ref[...]
    lane = lax.broadcasted_iota(jnp.int32, logits.shape, 1)
    inside = lane < classes
    top = jnp.max(jnp.where(inside, logits, -jnp.inf), 1, keepdims=True)
    shifted = jnp.where(inside, logits - top, 0.0)
    powers = jnp.where(inside, jnp.exp(shifted), 0.0)
    sum_powers = jnp.sum(powers, 1, keepdims=True)
    hot = hot_ref[...]
    losses = jnp.log(sum_powers) - jnp.sum(hot * shifted, 1, keepdims=True)
    single = (lax.broadcasted_iota(jnp.int32, (rows, 1), 0) % QUARTERS == 0).astype(f32)
    loss = jnp.sum(losses * weight * single, 0, keepdims=True)
    grad_low = ((weight / weight_total) * (powers / sum_powers - hot)).astype(bf16)
    grad_once = grad_low * single.astype(bf16)
    bias_grad = jnp.sum(grad_once.astype(f32), 0, keepdims=True)
    head_ref[...] = lax.dot_general(
        grad_once, pooled_low, (((0,), (0,)), ((), ())), preferred_element_type=f32
    )
    small_ref[...] = jnp.concatenate([bias_grad, jnp.broadcast_to(loss, (1, 128))], 0)
    spread = jnp.dot(grad_low, back_ref[...], preferred_element_type=f32) / count

    def scatter(J, carry):
        first_sum, second_sum = carry
        for s in range(NI):
            dy = spread * grads[s, J]
            dy_ref[s, J] = dy.astype(bf16)
            first_sum += by_eight(dy)
            second_sum += by_eight(dy * c_ref[s, J].astype(f32))
        return first_sum, second_sum

    zero = jnp.zeros((8, LANES), f32)
    first_sum, second_sum = lax.fori_loop(0, NJ, scatter, (zero, zero))
    first_sum = jnp.sum(first_sum, 0, keepdims=True)
    second_sum = (jnp.sum(second_sum, 0, keepdims=True) - mean * first_sum) * scale
    stat_ref[...] = jnp.broadcast_to(message(first_sum, second_sum), (devices, 128))


def grad_constants(sums_ref, gath_ref, counted, norm4, index):
    first_total, second_total = totals(sums_ref)
    mean, scale, slope, _ = norm_constants(gath_ref, counted, norm4, index)
    along = -slope * scale * second_total / counted
    return slope, along, -slope * first_total / counted - along * mean


def backward_kernel(*refs, index, residual, adding, devices):
    refs = list(refs)
    dy_ref, c_ref, prev_ref = refs[:3]
    refs = refs[3:]
    res_ref = refs.pop(0) if residual else None
    add_ref = refs.pop(0) if adding else None
    (
        sums_ref, gath_ref, gath_prev_ref, first_ref, norm_ref, mask_ref, q_ref, w_ref,
        out_ref, grad_ref, stat_ref, ring, side, vring, vside, slopes, sums, acc,
    ) = refs
    rows = c_ref.shape[2]
    counted = pixels_of(first_ref)
    grad_slope, grad_along, grad_start = grad_constants(
        sums_ref, gath_ref, counted, norm_ref, index
    )
    mean, scale, slope, start = norm_constants(gath_prev_ref, counted, norm_ref, index - 1)
    half_slope, half_start = slope * 0.5, start * 0.5
    lanes = half_lanes(rows)
    sums[...] = jnp.zeros_like(sums)
    acc[...] = jnp.zeros_like(acc)

    def activate(J, slot):
        Jc = jnp.minimum(J, NJ - 1)
        jm = mask_row(J)
        for s in range(NI):
            mask = twice(mask_ref[jm, 0 if s == 0 else 1])
            grad = (
                dy_ref[s, Jc].astype(f32) * grad_slope
                + c_ref[s, Jc].astype(f32) * grad_along
                + grad_start
            ) * mask
            put_column(ring, slot, s, grad, grad.astype(bf16), q_ref)
            half = prev_ref[s, Jc].astype(f32) * half_slope + half_start
            if residual:
                half = half + 0.5 * res_ref[s, Jc].astype(f32)
            t = jnp.tanh(half)
            value = (half + half * t) * mask
            put_column(vring, slot, s, value, value.astype(bf16), q_ref)
            slopes[slot, s] = (0.5 + 0.5 * t) * (1.0 + half * (1.0 - t)) * mask

    def convolve(J, u):
        side_columns(ring, side, u, lanes)
        side_columns(vring, vside, u, lanes)
        total = product(operands(ring, side, u), w_ref)
        first_sum, second_sum = sums[0], sums[1]
        for s in range(NI):
            tile = total[s * rows : (s + 1) * rows]
            if adding:
                tile = tile + add_ref[s, J].astype(f32)
            tile = tile * slopes[u + 1, s]
            out_ref[s, J] = tile.astype(bf16)
            first_sum += by_eight(tile)
            second_sum += by_eight(tile * prev_ref[s, J].astype(f32))
        sums[0], sums[1] = first_sum, second_sum

    ring[UNROLL] = jnp.zeros(ring.shape[1:], bf16)
    vring[UNROLL] = jnp.zeros(ring.shape[1:], bf16)
    for k in range(LAG):
        activate(k, UNROLL + 1 + k)

    def step(i, carry):
        for k in range(LAG + 1):
            ring[k] = ring[UNROLL + k]
            vring[k] = vring[UNROLL + k]
            slopes[k] = slopes[UNROLL + k]
        for u in range(UNROLL):
            activate(i * UNROLL + u + LAG, u + LAG + 1)
            convolve(i * UNROLL + u, u)
        grad = ring[1 : UNROLL + 1, 1 : NI + 1].reshape(UNROLL * NI * rows, LANES)
        parts = [operands(vring, vside, u) for u in range(UNROLL)]
        for k in range(4):
            value = jnp.concatenate([parts[u][k] for u in range(UNROLL)], 0)
            acc[:, k * LANES : (k + 1) * LANES] += lax.dot_general(
                grad, value, (((0,), (0,)), ((), ())), preferred_element_type=f32
            )
        return carry

    lax.fori_loop(0, NJ // UNROLL, step, 0)
    taps = [None] * 9
    for slot in range(16):
        for out in range(4):
            tap = tap_of(slot, out)
            if tap is not None:
                piece = acc[out * 64 : (out + 1) * 64, slot * 64 : (slot + 1) * 64]
                taps[tap] = piece if taps[tap] is None else taps[tap] + piece
    grad_ref[...] = jnp.concatenate(taps, 1)
    first_sum = jnp.sum(sums[0], 0, keepdims=True)
    second_sum = (jnp.sum(sums[1], 0, keepdims=True) - mean * first_sum) * scale
    stat_ref[...] = jnp.broadcast_to(message(first_sum, second_sum), (devices, 128))


def stem_back_kernel(
    dy_ref, c_ref, z_ref, sums_ref, gath_ref, norm_ref, mask_ref, grad_ref
):
    rows = c_ref.shape[2]
    counted = pixels_of(gath_ref)
    slope, along, start = grad_constants(sums_ref, gath_ref, counted, norm_ref, 0)
    span = 2 * NI
    deep = (span + 2) * 4
    total = jnp.zeros((4 * deep, NI * LANES), f32)
    for block in range(SIDE // span):
        for s in range(NI):
            at = (block * (span + 2) + 2 * s) * deep
            pieces = []
            for j in range(NI):
                J = block * NI + j
                mask = twice(mask_ref[0 if J < SHORT_J else 1, 0 if s == 0 else 1])
                pieces.append(
                    (
                        (
                            dy_ref[s, J].astype(f32) * slope
                            + c_ref[s, J].astype(f32) * along
                            + start
                        )
                        * mask
                    ).astype(bf16)
                )
            total += jnp.dot(
                z_ref[at : at + 4 * deep][:, :rows],
                jnp.concatenate(pieces, 1),
                preferred_element_type=f32,
            )
    grad_ref[...] = total


def stem_table():
    span = 2 * NI + 2
    table = np.zeros((NI * 4, 4, span, 4, 27), np.float32)
    for j in range(NI):
        for out in range(4):
            for ky in range(3):
                for kx in range(3):
                    for i in range(3):
                        table[
                            j * 4 + out, out // 2 + ky, 2 * j + out % 2 + kx, i,
                            (ky * 3 + kx) * 3 + i,
                        ] = 1.0
    return table.reshape(NI * 4, 4 * span * 4, 27)


def passed_along(value, axis, by):
    count = lax.axis_size(axis)
    return lax.ppermute(value, axis, [(i, (i + by) % count) for i in range(count)])


def flatten(stem, conv, norm, head, pieces):
    width = stem.shape[0] // pieces
    return jnp.concatenate(
        [
            stem.reshape(pieces, -1),
            conv.reshape(6, pieces, width, -1).transpose(1, 0, 2, 3).reshape(pieces, -1),
            norm.reshape(2, 7, pieces, width).transpose(2, 0, 1, 3).reshape(pieces, -1),
            head.reshape(head.shape[0], pieces, width).transpose(1, 0, 2).reshape(pieces, -1),
        ],
        1,
    )


def unflatten_one(share, width, channels, classes):
    first = width * 27
    second = first + 6 * width * 9 * channels
    third = second + 14 * width
    return (
        share[:first].reshape(width, 27),
        share[first:second].reshape(6, width, 9 * channels),
        share[second:third].reshape(2, 7, width),
        share[third:].reshape(classes, width),
    )


def quantize(block_value, noise):
    scale = jnp.max(jnp.abs(block_value), axis=-1, keepdims=True) + 1e-06
    dither = (noise.astype(jnp.float32) + 0.5) / 65536.0 - 0.5
    return (block_value / scale * levels + dither, scale)


def adam_update(gradient, first, second, master, factor):
    clipped = gradient * factor
    new_first = first_decay * first + (1.0 - first_decay) * clipped
    new_second = second_decay * second + (1.0 - second_decay) * clipped * clipped
    corrected = (
        new_first
        / (1.0 - first_decay**STEP)
        / (jnp.sqrt(new_second / (1.0 - second_decay**STEP)) + adam_epsilon)
    )
    return (master - learn_rate * (corrected + decoupled * master), new_first, new_second)


def shared(rows):
    return lax.all_to_all(rows, BOTH, 0, 0, tiled=True)


def body(
    images,
    large_flag,
    labels,
    example_weights,
    cycle_noise,
    stem_weight,
    conv_weight,
    norm_params,
    head_weight,
    head_bias,
    stem_first,
    stem_second,
    conv_first,
    conv_second,
    norm_first,
    norm_second,
    head_first,
    head_second,
    bias_first,
    bias_second,
):
    wide_count = lax.axis_size("wide")
    devices = wide_count * lax.axis_size("narrow")
    count = large_flag.shape[0]
    rows = QUARTERS * count
    width = stem_weight.shape[0]
    channels = width * wide_count
    classes = head_weight.shape[0]
    assert channels == 64 and rows % 16 == 0 and rows <= 128

    conv_full = lax.all_gather(conv_weight.astype(bf16), "wide", axis=1, tiled=True)
    small = jnp.concatenate(
        [stem_weight, norm_params.reshape(14, width).T, head_weight.T], 1
    )
    small = lax.all_gather(small, "wide", axis=0, tiled=True)
    stem_low = small[:, :27].astype(bf16)
    norm4 = jnp.tile(small[:, 27:41].T, (1, 4))
    norm4 = jnp.pad(norm4, ((0, 2), (0, 0)))
    head_low = small[:, 41:].astype(bf16)
    into_head = jnp.pad(head_low, ((0, 64), (0, 128 - classes)))
    from_head = jnp.pad(jnp.tile(head_low.T, (1, 4)), ((0, 128 - classes), (0, 0)))
    bias_row = jnp.pad(head_bias[None, :], ((0, 0), (0, 128 - classes)))
    stem_wide = jnp.einsum(
        "krt,ot->rko", jnp.asarray(stem_table(), bf16), stem_low, preferred_element_type=f32
    ).astype(bf16).reshape(-1, NI * LANES)

    large = large_flag == 1
    row_large = jnp.repeat(large, QUARTERS)
    quarter = jnp.arange(rows, dtype=jnp.int32) % QUARTERS
    upper = row_large | (quarter < SHORT_J // NI)
    ones = jnp.ones((rows,), bool)
    none = jnp.zeros((rows,), bool)
    mask_table = jnp.stack(
        [jnp.stack([ones, upper]), jnp.stack([row_large, row_large]), jnp.stack([none, none])]
    )
    mask_table = jnp.broadcast_to(mask_table[..., None], (3, 2, rows, 128)).astype(f32)
    q_table = jnp.broadcast_to(
        jnp.stack([quarter != QUARTERS - 1, quarter != 0])[..., None], (2, rows, 128)
    ).astype(f32)
    sides = jnp.where(large, SIDE, SHORT).astype(jnp.int32)
    weights_f = example_weights.astype(f32)
    lane = jnp.arange(128, dtype=jnp.int32)[None, :]
    info = jnp.where(
        lane == 0,
        jnp.repeat((sides * sides).astype(f32), QUARTERS)[:, None],
        jnp.where(lane == 1, jnp.repeat(weights_f, QUARTERS)[:, None], 0.0),
    )
    hot = (jnp.repeat(labels, QUARTERS)[:, None] == lane).astype(f32)

    span = 2 * NI
    position = jnp.arange(span * SIDE, dtype=jnp.int32)
    inside = row_large[:, None] | (
        (quarter[:, None] * span + (position // SIDE)[None, :] < SHORT)
        & ((position % SIDE)[None, :] < SHORT)
    )
    planes = images.reshape(3, rows, span * SIDE) * inside.astype(bf16)[None]

    big = jax.ShapeDtypeStruct((6, 1024, LANES), bf16)
    ahead, back = call(weights_kernel, (big, big), [], (conv_full,), "weights")

    z_rows = (SIDE // span) * (span + 2) * (span + 2) * 4
    ring_shape = (UNROLL + 1 + LAG, NI + 2, rows, LANES)
    side_shape = (UNROLL, NI + 2, rows, LANES)
    stat = jax.ShapeDtypeStruct((devices, 128), f32)

    c0, z, stat0 = call(
        functools.partial(stem_kernel, devices=devices),
        (
            field(rows),
            jax.ShapeDtypeStruct((z_rows, 128), bf16),
            jax.ShapeDtypeStruct((devices, LANES), f32),
        ),
        [pltpu.VMEM((z_rows, 128), f32)],
        (planes, stem_wide, mask_table, info),
        "stem",
    )
    fields = [c0]
    gathered = [shared(stat0)]
    streams = []
    for layer in range(1, 7):
        keep = layer % 2 == 1
        residual = keep and layer > 1
        args = (fields[layer - 1],) + ((streams[-1],) if residual else ())
        args += (gathered[layer - 1], gathered[0], norm4, mask_table, q_table, ahead[layer - 1])
        outs = call(
            functools.partial(
                forward_kernel, index=layer - 1, keep=keep, residual=residual, devices=devices
            ),
            (field(rows),) + ((field(rows),) if keep else ()) + (stat,),
            [
                pltpu.VMEM(ring_shape, bf16),
                pltpu.VMEM(side_shape, bf16),
                pltpu.VMEM((2, 8, LANES), f32),
            ],
            args,
            "forward",
        )
        fields.append(outs[0])
        if keep:
            streams.append(outs[1])
        gathered.append(shared(outs[-1]))

    dys = [None] * 7
    stats = [None] * 7
    dys[6], stats[6], head_grad, small_grads = call(
        functools.partial(head_kernel, classes=classes, devices=devices),
        (
            field(rows),
            stat,
            jax.ShapeDtypeStruct((128, 128), f32),
            jax.ShapeDtypeStruct((2, 128), f32),
        ),
        [pltpu.VMEM((NI, NJ, rows, LANES), f32), pltpu.VMEM((rows, LANES), f32)],
        (
            fields[6], streams[2], gathered[6], gathered[0], norm4, mask_table, hot, info,
            into_head, from_head, bias_row,
        ),
        "head",
    )
    conv_grads = [None] * 6
    for layer in range(6, 0, -1):
        residual = layer in (5, 3)
        adding = layer % 2 == 1
        sums = shared(stats[layer])
        args = (dys[layer], fields[layer], fields[layer - 1])
        args += (streams[layer // 2 - 1],) if residual else ()
        args += (dys[layer + 1],) if adding else ()
        args += (
            sums, gathered[layer], gathered[layer - 1], gathered[0], norm4, mask_table, q_table,
            back[layer - 1],
        )
        dys[layer - 1], conv_grads[layer - 1], stats[layer - 1] = call(
            functools.partial(
                backward_kernel, index=layer, residual=residual, adding=adding, devices=devices
            ),
            (field(rows), jax.ShapeDtypeStruct((64, 576), f32), stat),
            [
                pltpu.VMEM(ring_shape, bf16),
                pltpu.VMEM(side_shape, bf16),
                pltpu.VMEM(ring_shape, bf16),
                pltpu.VMEM(side_shape, bf16),
                pltpu.VMEM((UNROLL + 1 + LAG, NI, rows, LANES), f32),
                pltpu.VMEM((2, 8, LANES), f32),
                pltpu.VMEM((LANES, 1024), f32),
            ],
            args,
            "backward",
        )
    stem_raw = call(
        stem_back_kernel,
        jax.ShapeDtypeStruct((4 * (span + 2) * 4, NI * LANES), f32),
        [],
        (dys[0], fields[0], z, shared(stats[0]), gathered[0], norm4, mask_table),
        "stem_back",
    )
    stem_grad = jnp.einsum(
        "krt,rko->ot",
        jnp.asarray(stem_table(), f32),
        stem_raw.reshape(-1, NI * 4, 64),
        precision=lax.Precision.HIGHEST,
    )
    local = jnp.stack([s[0] for s in stats])
    norm_grad = jnp.stack([local[:, 64:], local[:, :64]])
    conv_grad = jnp.stack(conv_grads, 0)
    head_grad = head_grad[:classes, :64]
    bias_grad = small_grads[0, :classes]
    loss_part = small_grads[1, 0]
    weight_total = jnp.sum(gathered[0][:, 129])

    member = lax.axis_index("wide")
    flat = flatten(stem_grad, conv_grad, norm_grad, head_grad, wide_count)
    flat, bias_sum, loss_narrow = (
        lax.psum(flat.astype(jnp.bfloat16), "narrow").astype(jnp.float32),
        lax.psum(bias_grad.astype(jnp.bfloat16), "narrow").astype(jnp.float32),
        lax.psum(loss_part.astype(jnp.bfloat16), "narrow").astype(jnp.float32),
    )

    def own_row(row):
        piece = lax.dynamic_index_in_dim(flat, (row + 2 * wide_count) % wide_count, 0, False)
        return piece

    def one_hop(hop, carried):
        noise = lax.dynamic_index_in_dim(cycle_noise[0], hop - 1, 0, False)
        level, scale = quantize(carried, noise)
        level_in = passed_along(level.astype(jnp.bfloat16), "wide", 1)
        scale_in = passed_along(scale, "wide", 1)
        return level_in.astype(jnp.float32) * scale_in / levels + own_row(member - 1 - hop)

    reduced = lax.fori_loop(1, wide_count, one_hop, own_row(member - 1))
    stem_share, conv_share, norm_share, head_share = unflatten_one(
        reduced, stem_weight.shape[0], channels, classes
    )
    stem_share = stem_share + weight_decay * stem_weight
    conv_share = conv_share + weight_decay * conv_weight
    head_share = head_share + weight_decay * head_weight
    squares = (
        jnp.sum(stem_share * stem_share)
        + jnp.sum(conv_share * conv_share)
        + jnp.sum(norm_share * norm_share)
        + jnp.sum(head_share * head_share)
    )
    square_total, bias_total, loss_total = lax.psum((squares, bias_sum, loss_narrow), "wide")
    grad_norm = jnp.sqrt(square_total + jnp.sum(bias_total * bias_total))
    factor = clip_limit / jnp.maximum(grad_norm, clip_limit)
    results = []
    for gradient, first, second, master in (
        (stem_share, stem_first, stem_second, stem_weight),
        (conv_share, conv_first, conv_second, conv_weight),
        (norm_share, norm_first, norm_second, norm_params),
        (head_share, head_first, head_second, head_weight),
        (bias_total, bias_first, bias_second, head_bias),
    ):
        results.extend(adam_update(gradient, first, second, master, factor))
    return (*results, grad_norm, loss_total, weight_total)


def solution(mesh):
    split = P(BOTH)
    ins = (
        P(None, BOTH), split, split, split, P("wide", None, None),
        P("wide", None), P(None, "wide", None), P(None, None, "wide"), P(None, "wide"), P(),
        P("wide", None), P("wide", None), P(None, "wide", None), P(None, "wide", None),
        P(None, None, "wide"), P(None, None, "wide"), P(None, "wide"), P(None, "wide"), P(), P(),
    )
    outs = (
        (P("wide", None),) * 3
        + (P(None, "wide", None),) * 3
        + (P(None, None, "wide"),) * 3
        + (P(None, "wide"),) * 3
        + (P(),) * 6
    )
    return jax.shard_map(body, mesh=mesh, in_specs=ins, out_specs=outs, check_vma=False)
```

time: 2070 us -> 565 us (0.27)
  other arithmetic: 839 us -> 29.7 us
  blocking collectives: 666 us -> 118 us
  matrix products: 398 us -> 3.5 us
  Pallas kernels: 0 us -> 257 us
  local copies, waits for them, and re-layouts: 71.6 us -> 22.6 us
  waiting for transfers between devices: 47.8 us -> 73.6 us
    psum x15 -> x0, blocking collectives: 600 us -> none  [the longest x7 281 us: norm_backward(): lax.psum((shift_local, gain_local), ('wide', 'narrow'))]
    dot_general x23 -> x2, matrix products: 398 us -> 3.5 us  [the longest x1 2.23 us: body(): jnp.einsum('krt,rko->ot', jnp.asarray(stem_table(), f32), stem_raw.reshap...]
    mul x26 -> x2, other arithmetic: 280 us -> 0.03 us  [the longest x1 0.02 us: body(): planes = images.reshape(3, rows, span * SIDE) * inside.astype(bf16)[None]]
    pallas_call x0 -> x16, Pallas kernels: none -> 257 us  [call(): pl.pallas_call(kernel, out_shape=outs, in_specs=[whole()] * len(args), ou...]
    reduce_sum x12 -> x1, other arithmetic: 227 us -> 0.67 us  [body(): weight_total = jnp.sum(gathered[0][:, 129])]
    unnamed x52 -> x5, other arithmetic: 166 us -> 0.09 us
    convert_element_type x19 -> x7, other arithmetic: 99.6 us -> 1.63 us  [the longest x1 0.7 us: body(): (sides * sides).astype(f32)]
    all_to_all x0 -> x8, blocking collectives: none -> 74.6 us  [shared(): return lax.all_to_all(rows, BOTH, 0, 0, tiled=True)]
  transfers between devices with their start and end apart: 15 -> 21, of which waited for: 8 -> 13; matrix products, arithmetic and copies ran while one was open for 0% -> 2% of each run, Pallas kernels for 0% -> 1%
where the time goes in v1:
time: 565 us; the launch traced here: 556 us
  Pallas kernels  257 us (45%)
  blocking collectives  118 us (21%)
  waiting for transfers between devices  73.6 us (13%)
  other arithmetic  29.7 us (5%)
  starting transfers between devices  26.9 us (5%)
  local copies, waits for them, and re-layouts  22.6 us (4%)
  between operations  20.2 us (4%)
    pallas_call x16, Pallas kernels, call(): pl.pallas_call(kernel, out_shape=outs, in_specs=[whole()] * len(args), ou...  257 us
    all_to_all x8, blocking collectives, shared(): return lax.all_to_all(rows, BOTH, 0, 0, tiled=True)  74.6 us
    all_to_all x6, waiting for transfers between devices, shared(): return lax.all_to_all(rows, BOTH, 0, 0, tiled=True)  29.2 us
    psum x1, waiting for transfers between devices, body(): lax.psum(flat.astype(jnp.bfloat16), 'narrow').astype(jnp.float32)  23.2 us
    ppermute x14, waiting for transfers between devices, passed_along(): lax.ppermute(value, axis, [(i, (i + by) % count) for i in range(count)])  21.1 us
    all_to_all x6, starting transfers between devices, shared(): return lax.all_to_all(rows, BOTH, 0, 0, tiled=True)  17.9 us
    psum x1, blocking collectives, body(): lax.psum((squares, bias_sum, loss_narrow), 'wide')  12.9 us
  transfers between devices with their start and end apart: 21, of which 13 were waited for; matrix products, arithmetic and copies ran while one was open for 2% of the time, Pallas kernels for 1%

profile of v1, /device:TPU:0, one launch (start us, length us, event | category | flops | bytes accessed | tf_op | source)
XLA Modules:
  0.0 556.2 jit_solution(11185153017132834831)
XLA Ops:
  11.6 10.5 %all_gather.6 = f32[64,51]{1,0:T(8,128)S(1)} all-gather(f32[8,51]{1,0:T(8,128)S(1)} %pad_maximum_fusion), channel_id=1, replica_groups=mesh['wide'=8,'narrow'=4] {'wide'}, dimensions={0}, use_global_device_ids=true | all-gather | bytes 14688 | tf_op jit(solution)/shard_map/all_gather | solution.py:617
  36.5 10.3 %all_gather.7.conv_ref = bf16[6,64,576]{2,1,0:T(8,128)(2,1)S(1)} all-gather(bf16[6,8,576]{2,1,0:T(8,128)(2,1)S(1)} %convert_element_type.109), channel_id=1, replica_groups=mesh['wide'=8,'narrow'=4] {'wide'}, dimensions={1}, use_global_device_ids=true | all-gather | bytes 497664 | tf_op jit(solution)/shard_map/all_gather | solution.py:613
  54.3 19.4 %forward.6 = (bf16[5,20,80,256]{3,2,1,0:T(8,128)(2,1)}, bf16[5,20,80,256]{3,2,1,0:T(8,128)(2,1)}, f32[32,128]{1,0:T(8,128)S(1)}) custom-call(bf16[5,20,80,256]{3,2,1,0:T(8,128)(2,1)} %get-tuple-element.259.refs_0_.refs_2_.c_ref, f32[32,256]{1,0:T(8,128)S(1)} %bitcast.135, f32[32,256]{1,0:T(8,128)S(1)} %bitcast.136, ...), custom_call_target="tpu_custom_call" | custom-call | tf_op jit(solution)/shard_map/forward/pallas_call | solution.py:60
  73.7 11.6 %all_to_all.154 = f32[32,1,128]{2,1,0:T(1,128)S(1)} all-to-all(f32[32,1,128]{2,1,0:T(1,128)S(1)} %bitcast.181), channel_id=1, replica_groups=mesh['wide'=8,'narrow'=4] {'wide','narrow'}, dimensions={0} | all-to-all | bytes 32768 | tf_op jit(solution)/shard_map/all_to_all | solution.py:579
  85.3 10.7 %forward.7 = (bf16[5,20,80,256]{3,2,1,0:T(8,128)(2,1)}, f32[32,128]{1,0:T(8,128)S(1)}) custom-call(bf16[5,20,80,256]{3,2,1,0:T(8,128)(2,1)} %get-tuple-element.262.refs_0_.refs_2_.refs_1_, f32[32,128]{1,0:T(8,128)S(1)} %bitcast.152, f32[32,256]{1,0:T(8,128)S(1)} %bitcast.137, f32[16,256]{1,0:T(8,128)S(1)} %pad.17.refs_3_.refs_4_.norm_ref.refs_7_.refs_9_.refs_8_, ...), custom_call_target="tpu_custom_call" | custom-call | tf_op jit(solution)/shard_map/forward/pallas_call | solution.py:60
  96.0 9.4 %all_to_all.155 = f32[32,1,128]{2,1,0:T(1,128)S(1)} all-to-all(f32[32,1,128]{2,1,0:T(1,128)S(1)} %bitcast.183), channel_id=1, replica_groups=mesh['wide'=8,'narrow'=4] {'wide','narrow'}, dimensions={0} | all-to-all | bytes 32768 | tf_op jit(solution)/shard_map/all_to_all | solution.py:579
  105.4 21.7 %forward.8 = (bf16[5,20,80,256]{3,2,1,0:T(8,128)(2,1)}, bf16[5,20,80,256]{3,2,1,0:T(8,128)(2,1)}, f32[32,128]{1,0:T(8,128)S(1)}) custom-call(bf16[5,20,80,256]{3,2,1,0:T(8,128)(2,1)} %get-tuple-element.264.refs_0_.refs_2_.refs_1_, bf16[5,20,80,256]{3,2,1,0:T(8,128)(2,1)} %get-tuple-element.265.refs_1_.refs_3_, f32[32,128]{1,0:T(8,128)S(1)} %bitcast.155, ...), custom_call_target="tpu_custom_call" | custom-call | tf_op jit(solution)/shard_map/forward/pallas_call | solution.py:60
  127.0 8.8 %all_to_all.156 = f32[32,1,128]{2,1,0:T(1,128)S(1)} all-to-all(f32[32,1,128]{2,1,0:T(1,128)S(1)} %bitcast.182), channel_id=1, replica_groups=mesh['wide'=8,'narrow'=4] {'wide','narrow'}, dimensions={0} | all-to-all | bytes 32768 | tf_op jit(solution)/shard_map/all_to_all | solution.py:579
  135.9 10.7 %forward.9 = (bf16[5,20,80,256]{3,2,1,0:T(8,128)(2,1)}, f32[32,128]{1,0:T(8,128)S(1)}) custom-call(bf16[5,20,80,256]{3,2,1,0:T(8,128)(2,1)} %get-tuple-element.267.refs_0_.refs_2_.refs_1_, f32[32,128]{1,0:T(8,128)S(1)} %bitcast.158, f32[32,256]{1,0:T(8,128)S(1)} %bitcast.139, f32[16,256]{1,0:T(8,128)S(1)} %pad.17.refs_3_.refs_4_.norm_ref.refs_7_.refs_9_.refs_8_, ...), custom_call_target="tpu_custom_call" | custom-call | tf_op jit(solution)/shard_map/forward/pallas_call | solution.py:60
  146.6 8.8 %all_to_all.157 = f32[32,1,128]{2,1,0:T(1,128)S(1)} all-to-all(f32[32,1,128]{2,1,0:T(1,128)S(1)} %bitcast.184), channel_id=1, replica_groups=mesh['wide'=8,'narrow'=4] {'wide','narrow'}, dimensions={0} | all-to-all | bytes 32768 | tf_op jit(solution)/shard_map/all_to_all | solution.py:579
  155.5 21.6 %forward.10 = (bf16[5,20,80,256]{3,2,1,0:T(8,128)(2,1)}, bf16[5,20,80,256]{3,2,1,0:T(8,128)(2,1)}, f32[32,128]{1,0:T(8,128)}) custom-call(bf16[5,20,80,256]{3,2,1,0:T(8,128)(2,1)} %get-tuple-element.269.refs_0_.refs_2_.refs_1_, bf16[5,20,80,256]{3,2,1,0:T(8,128)(2,1)} %get-tuple-element.270.refs_1_.refs_3_, f32[32,128]{1,0:T(8,128)S(1)} %bitcast.161, ...), custom_call_target="tpu_custom_call" | custom-call | tf_op jit(solution)/shard_map/forward/pallas_call | solution.py:60
  180.0 6.8 %all-to-all-done.5 = f32[32,1,128]{2,1,0:T(1,128)S(1)} async-done(((f32[32,1,128]{2,1,0:T(1,128)}), f32[32,1,128]{2,1,0:T(1,128)S(1)}, u32[]{:S(2)}, u32[]{:S(2)}) %all-to-all-start.5) | async-done | bytes 16416 | tf_op jit(solution)/shard_map/all_to_all | solution.py:579
  186.9 10.7 %forward.11 = (bf16[5,20,80,256]{3,2,1,0:T(8,128)(2,1)}, f32[32,128]{1,0:T(8,128)}) custom-call(bf16[5,20,80,256]{3,2,1,0:T(8,128)(2,1)} %get-tuple-element.272.refs_0_.refs_2_.refs_1_, f32[32,128]{1,0:T(8,128)S(1)} %bitcast.164, f32[32,256]{1,0:T(8,128)S(1)} %bitcast.141, f32[16,256]{1,0:T(8,128)S(1)} %pad.17.refs_3_.refs_4_.norm_ref.refs_7_.refs_9_.refs_8_, ...), custom_call_target="tpu_custom_call" | custom-call | tf_op jit(solution)/shard_map/forward/pallas_call | solution.py:60
  200.5 6.8 %all-to-all-done.6 = f32[32,1,128]{2,1,0:T(1,128)S(1)} async-done(((f32[32,1,128]{2,1,0:T(1,128)}), f32[32,1,128]{2,1,0:T(1,128)S(1)}, u32[]{:S(2)}, u32[]{:S(2)}) %all-to-all-start.6) | async-done | bytes 16416 | tf_op jit(solution)/shard_map/all_to_all | solution.py:579
  207.3 12.6 %head.1 = (bf16[5,20,80,256]{3,2,1,0:T(8,128)(2,1)}, f32[32,128]{1,0:T(8,128)}, f32[128,128]{1,0:T(8,128)S(1)}, f32[2,128]{1,0:T(2,128)S(1)}) custom-call(bf16[5,20,80,256]{3,2,1,0:T(8,128)(2,1)} %get-tuple-element.274.c_ref.refs_1_, bf16[5,20,80,256]{3,2,1,0:T(8,128)(2,1)} %get-tuple-element.275.res_ref, f32[32,128]{1,0:T(8,128)S(1)} %bitcast.167, ...), custom_call_target="tpu_custom_call" | custom-call | tf_op jit(solution)/shard_map/head/pallas_call | solution.py:60
  229.7 21.1 %backward.6 = (bf16[5,20,80,256]{3,2,1,0:T(8,128)(2,1)}, f32[64,576]{1,0:T(8,128)S(1)}, f32[32,128]{1,0:T(8,128)S(1)}) custom-call(bf16[5,20,80,256]{3,2,1,0:T(8,128)(2,1)} %get-tuple-element.277.refs_0_.refs_4_, bf16[5,20,80,256]{3,2,1,0:T(8,128)(2,1)} %get-tuple-element.274.c_ref.refs_1_, ...), custom_call_target="tpu_custom_call" | custom-call | tf_op jit(solution)/shard_map/backward/pallas_call | solution.py:60
  250.8 8.8 %all_to_all.158 = f32[32,1,128]{2,1,0:T(1,128)S(1)} all-to-all(f32[32,1,128]{2,1,0:T(1,128)S(1)} %bitcast.177), channel_id=1, replica_groups=mesh['wide'=8,'narrow'=4] {'wide','narrow'}, dimensions={0} | all-to-all | bytes 32768 | tf_op jit(solution)/shard_map/all_to_all | solution.py:579
  259.7 24.8 %backward.7 = (bf16[5,20,80,256]{3,2,1,0:T(8,128)(2,1)}, f32[64,576]{1,0:T(8,128)S(1)}, f32[32,128]{1,0:T(8,128)S(1)}) custom-call(bf16[5,20,80,256]{3,2,1,0:T(8,128)(2,1)} %get-tuple-element.280.refs_0_, bf16[5,20,80,256]{3,2,1,0:T(8,128)(2,1)} %get-tuple-element.272.refs_0_.refs_2_.refs_1_, ...), custom_call_target="tpu_custom_call" | custom-call | tf_op jit(solution)/shard_map/backward/pallas_call | solution.py:60
  284.5 9.1 %all_to_all.159 = f32[32,1,128]{2,1,0:T(1,128)S(1)} all-to-all(f32[32,1,128]{2,1,0:T(1,128)S(1)} %bitcast.178), channel_id=1, replica_groups=mesh['wide'=8,'narrow'=4] {'wide','narrow'}, dimensions={0} | all-to-all | bytes 32768 | tf_op jit(solution)/shard_map/all_to_all | solution.py:579
  293.6 21.1 %backward.8 = (bf16[5,20,80,256]{3,2,1,0:T(8,128)(2,1)}, f32[64,576]{1,0:T(8,128)S(1)}, f32[32,128]{1,0:T(8,128)S(1)}) custom-call(bf16[5,20,80,256]{3,2,1,0:T(8,128)(2,1)} %get-tuple-element.282.refs_0_.refs_4_, bf16[5,20,80,256]{3,2,1,0:T(8,128)(2,1)} %get-tuple-element.269.refs_0_.refs_2_.refs_1_, ...), custom_call_target="tpu_custom_call" | custom-call | tf_op jit(solution)/shard_map/backward/pallas_call | solution.py:60
  314.7 8.8 %all_to_all.160 = f32[32,1,128]{2,1,0:T(1,128)S(1)} all-to-all(f32[32,1,128]{2,1,0:T(1,128)S(1)} %bitcast.179), channel_id=1, replica_groups=mesh['wide'=8,'narrow'=4] {'wide','narrow'}, dimensions={0} | all-to-all | bytes 32768 | tf_op jit(solution)/shard_map/all_to_all | solution.py:579
  323.5 24.8 %backward.9 = (bf16[5,20,80,256]{3,2,1,0:T(8,128)(2,1)}, f32[64,576]{1,0:T(8,128)S(1)}, f32[32,128]{1,0:T(8,128)S(1)}) custom-call(bf16[5,20,80,256]{3,2,1,0:T(8,128)(2,1)} %get-tuple-element.284.refs_0_, bf16[5,20,80,256]{3,2,1,0:T(8,128)(2,1)} %get-tuple-element.267.refs_0_.refs_2_.refs_1_, ...), custom_call_target="tpu_custom_call" | custom-call | tf_op jit(solution)/shard_map/backward/pallas_call | solution.py:60
  348.4 9.2 %all_to_all.161 = f32[32,1,128]{2,1,0:T(1,128)S(1)} all-to-all(f32[32,1,128]{2,1,0:T(1,128)S(1)} %bitcast.180), channel_id=1, replica_groups=mesh['wide'=8,'narrow'=4] {'wide','narrow'}, dimensions={0} | all-to-all | bytes 32768 | tf_op jit(solution)/shard_map/all_to_all | solution.py:579
  357.5 21.1 %backward.10 = (bf16[5,20,80,256]{3,2,1,0:T(8,128)(2,1)}, f32[64,576]{1,0:T(8,128)S(1)}, f32[32,128]{1,0:T(8,128)}) custom-call(bf16[5,20,80,256]{3,2,1,0:T(8,128)(2,1)} %get-tuple-element.286.refs_0_.refs_3_, bf16[5,20,80,256]{3,2,1,0:T(8,128)(2,1)} %get-tuple-element.264.refs_0_.refs_2_.refs_1_, ...), custom_call_target="tpu_custom_call" | custom-call | tf_op jit(solution)/shard_map/backward/pallas_call | solution.py:60
  382.8 5.5 all-to-all-done.12
  388.3 22.8 %backward.11 = (bf16[5,20,80,256]{3,2,1,0:T(8,128)(2,1)}, f32[64,576]{1,0:T(8,128)S(1)}, f32[32,128]{1,0:T(8,128)}) custom-call(bf16[5,20,80,256]{3,2,1,0:T(8,128)(2,1)} %get-tuple-element.288.refs_0_, bf16[5,20,80,256]{3,2,1,0:T(8,128)(2,1)} %get-tuple-element.262.refs_0_.refs_2_.refs_1_, bf16[5,20,80,256]{3,2,1,0:T(8,128)(2,1)} %get-tuple-element.259.refs_0_.refs_2_.c_ref, ...), custom_call_target="tpu_custom_call" | custom-call | tf_op jit(solution)/shard_map/backward/pallas_call | solution.py:60
  415.7 5.8 %all-to-all-done.13 = f32[32,1,128]{2,1,0:T(1,128)S(1)} async-done(((f32[32,1,128]{2,1,0:T(1,128)}), f32[32,1,128]{2,1,0:T(1,128)S(1)}, u32[]{:S(2)}, u32[]{:S(2)}) %all-to-all-start.13) | async-done | bytes 16416 | tf_op jit(solution)/shard_map/all_to_all | solution.py:579
  421.5 6.2 %stem_back.1 = f32[192,1280]{1,0:T(8,128)S(1)} custom-call(bf16[5,20,80,256]{3,2,1,0:T(8,128)(2,1)} %get-tuple-element.290.dy_ref, bf16[5,20,80,256]{3,2,1,0:T(8,128)(2,1)} %get-tuple-element.259.refs_0_.refs_2_.c_ref, bf16[2304,128]{1,0:T(8,128)(2,1)S(1)} %copy-done.3, f32[32,128]{1,0:T(8,128)S(1)} %bitcast.169, f32[32,256]{1,0:T(8,128)S(1)} %bitcast.150, ...), custom_call_target="tpu_custom_call" | custom-call | tf_op jit(solution)/shard_map/stem_back/pallas_call | solution.py:60
  433.1 9.5 %all-reduce.6 = (bf16[10]{0:T(256)(128)(2,1)S(1)}, bf16[]{:T(256)}) all-reduce(bf16[10]{0:T(256)(128)(2,1)S(1)} %slice_bitcast_fusion.15, bf16[]{:T(256)} %bitcast.76), channel_id=1, replica_groups=mesh['wide'=8,'narrow'=4] {'narrow'}, use_global_device_ids=true, to_apply=%region_9.10 | all-reduce | flops 11 | bytes 44 | tf_op jit(solution)/shard_map/psum | solution.py:776
  442.6 23.2 %all-reduce.9.cloned.1.call-done = bf16[8,28056]{1,0:T(8,128)(2,1)} async-done(((bf16[8,28056]{1,0:T(8,128)(2,1)}), bf16[8,28056]{1,0:T(8,128)(2,1)}) %all-reduce.9.cloned.1.call-update) | async-done | bytes 448912 | tf_op jit(solution)/shard_map/psum | solution.py:775
  467.8 54.8 %while.18 = (s32[]{:T(128)}, f32[28056]{0:T(1024)S(1)}, s32[1,7,28056]{2,0,1:T(1,128)}, s32[]{:T(128)}, f32[8,28056]{1,0:T(8,128)S(1)}, /*index=5*/f32[]{:T(128)...) while((s32[]{:T(128)}, f32[28056]{0:T(1024)S(1)}, ...), condition=%wide.region_3.4_spmd, body=%wide.region_1.3_spmd.sunk | while | flops 392802 | bytes 1234876 | solution.py:791
  528.3 12.9 %all-reduce.5 = (f32[]{:T(128)}, f32[10]{0:T(128)S(1)}, f32[]{:T(128)}) all-reduce(f32[]{:T(128)S(6)} %add.376, bf16[10]{0:T(256)(128)(2,1)S(1)} %get-tuple-element.415, bf16[]{:T(256)} %get-tuple-element.416), channel_id=1, replica_groups=mesh['wide'=8,'narrow'=4] {'wide'}, use_global_device_ids=true, to_apply=%region_8.9 | all-reduce | flops 12 | bytes 74 | tf_op jit(solution)/shard_map/psum | solution.py:804
  (223 shorter events, 115.9 us)
Async XLA Ops:
  31.3 21.9 %all-to-all-start = ((f32[32,1,256]{2,1,0:T(1,128)}), f32[32,1,256]{2,1,0:T(1,128)S(1)}, u32[]{:S(2)}, u32[]{:S(2)}) async-start(f32[32,1,256]{2,1,0:T(1,128)} %copy.133), calls=%async_computation | async-start | bytes 65536 | tf_op jit(solution)/shard_map/all_to_all | solution.py:579
  177.1 9.8 %all-to-all-start.5 = ((f32[32,1,128]{2,1,0:T(1,128)}), f32[32,1,128]{2,1,0:T(1,128)S(1)}, u32[]{:S(2)}, u32[]{:S(2)}) async-start(f32[32,1,128]{2,1,0:T(1,128)} %bitcast.29), calls=%async_computation.5 | async-start | bytes 32768 | tf_op jit(solution)/shard_map/all_to_all | solution.py:579
  197.6 9.6 %all-to-all-start.6 = ((f32[32,1,128]{2,1,0:T(1,128)}), f32[32,1,128]{2,1,0:T(1,128)S(1)}, u32[]{:S(2)}, u32[]{:S(2)}) async-start(f32[32,1,128]{2,1,0:T(1,128)} %bitcast.33), calls=%async_computation.6 | async-start | bytes 32768 | tf_op jit(solution)/shard_map/all_to_all | solution.py:579
  219.8 9.9 %all-to-all-start.7 = ((f32[32,1,128]{2,1,0:T(1,128)}), f32[32,1,128]{2,1,0:T(1,128)S(1)}, u32[]{:S(2)}, u32[]{:S(2)}) async-start(f32[32,1,128]{2,1,0:T(1,128)} %bitcast.38), calls=%async_computation.7 | async-start | bytes 32768 | tf_op jit(solution)/shard_map/all_to_all | solution.py:579
  378.6 9.6 %all-to-all-start.12 = ((f32[32,1,128]{2,1,0:T(1,128)}), f32[32,1,128]{2,1,0:T(1,128)S(1)}, u32[]{:S(2)}, u32[]{:S(2)}) async-start(f32[32,1,128]{2,1,0:T(1,128)} %bitcast.58), calls=%async_computation.12 | async-start | bytes 32768 | tf_op jit(solution)/shard_map/all_to_all | solution.py:579
  411.9 9.6 %all-to-all-start.13 = ((f32[32,1,128]{2,1,0:T(1,128)}), f32[32,1,128]{2,1,0:T(1,128)S(1)}, u32[]{:S(2)}, u32[]{:S(2)}) async-start(f32[32,1,128]{2,1,0:T(1,128)} %bitcast.62), calls=%async_computation.13 | async-start | bytes 32768 | tf_op jit(solution)/shard_map/all_to_all | solution.py:579
  414.4 51.4 %all-reduce.9.cloned.1.call-start = ((), (), s32[]{:S(2)}) async-start(), calls=%async_computation.14 | async-start | bytes 901120 | tf_op jit(solution)/shard_map/psum | solution.py:775
  431.8 111.5 %copy-start.10 = (f32[2,7,8]{2,0,1:T(2,128)S(1)}, f32[2,7,8]{2,0,1:T(2,128)}, u32[]{:S(2)}) copy-start(f32[2,7,8]{2,0,1:T(2,128)} %param.31) | copy-start | bytes 1348
  431.8 111.5 %copy-start.11 = (f32[2,7,8]{2,0,1:T(2,128)S(1)}, f32[2,7,8]{2,0,1:T(2,128)}, u32[]{:S(2)}) copy-start(f32[2,7,8]{2,0,1:T(2,128)} %param.38) | copy-start | bytes 1348
  431.8 111.5 %copy-start.12 = (f32[2,7,8]{2,0,1:T(2,128)S(1)}, f32[2,7,8]{2,0,1:T(2,128)}, u32[]{:S(2)}) copy-start(f32[2,7,8]{2,0,1:T(2,128)} %param.39) | copy-start | bytes 1348
  432.5 112.6 %copy-start.19 = (f32[10]{0:T(128)S(1)}, f32[10]{0:T(128)}, u32[]{:S(2)}) copy-start(f32[10]{0:T(128)} %param.42) | copy-start | bytes 124
  432.5 112.6 %copy-start.20 = (f32[10]{0:T(128)S(1)}, f32[10]{0:T(128)}, u32[]{:S(2)}) copy-start(f32[10]{0:T(128)} %param.43) | copy-start | bytes 124
  432.5 113.1 %copy-start.13 = (f32[10,8]{0,1:T(8,128)S(1)}, f32[10,8]{0,1:T(8,128)}, u32[]{:S(2)}) copy-start(f32[10,8]{0,1:T(8,128)} %param.40) | copy-start | bytes 964
  432.5 113.1 %copy-start.14 = (f32[10,8]{0,1:T(8,128)S(1)}, f32[10,8]{0,1:T(8,128)}, u32[]{:S(2)}) copy-start(f32[10,8]{0,1:T(8,128)} %param.41) | copy-start | bytes 964
  442.6 103.7 %copy-start.15 = (f32[8,27]{1,0:T(8,128)S(1)}, f32[8,27]{1,0:T(8,128)}, u32[]{:S(2)}) copy-start(f32[8,27]{1,0:T(8,128)} %param.34) | copy-start | bytes 2596
  442.6 103.7 %copy-start.16 = (f32[8,27]{1,0:T(8,128)S(1)}, f32[8,27]{1,0:T(8,128)}, u32[]{:S(2)}) copy-start(f32[8,27]{1,0:T(8,128)} %param.35) | copy-start | bytes 2596
  442.6 104.3 %copy-start.6 = (f32[6,8,576]{2,1,0:T(8,128)S(1)}, f32[6,8,576]{2,1,0:T(8,128)}, u32[]{:S(2)}) copy-start(f32[6,8,576]{2,1,0:T(8,128)} %param.36) | copy-start | bytes 331780
  442.6 104.3 %copy-start.7 = (f32[6,8,576]{2,1,0:T(8,128)S(1)}, f32[6,8,576]{2,1,0:T(8,128)}, u32[]{:S(2)}) copy-start(f32[6,8,576]{2,1,0:T(8,128)} %param.37) | copy-start | bytes 331780
  469.8 4.6 collective-permute-start.1
  469.9 4.5 collective-permute-start
  477.6 4.6 collective-permute-start.1
  477.7 4.5 collective-permute-start
  485.5 4.6 collective-permute-start.1
  485.5 4.5 collective-permute-start
  493.3 4.6 collective-permute-start.1
  493.4 4.5 collective-permute-start
  501.1 4.6 collective-permute-start.1
  501.2 4.5 collective-permute-start
  508.9 4.6 collective-permute-start.1
  509.0 4.5 collective-permute-start
  516.8 4.6 collective-permute-start.1
  516.8 4.5 collective-permute-start
  (10 other events, 419.5 us)
Sparse Core Ops, SparseCore 0:
  431.9 33.8 all-reduce.8
